TPU v7x, 256 devices: a whole 4x4x8 slice. The times are simulated.
256 devices in a mesh: context: 16 (over y, z_hi, core), tensor: 16 (over z_lo, x).
Axes of the slice: x: 4, y: 4, z: 8 (z_hi: 2, z_lo: 4; z = z_hi * 4 + z_lo), core: 2. Of those that a mesh axis runs over, the one named last changes fastest.
Arguments:
- queries: bfloat16 [2048, 6144], P('context', 'tensor')
- context_keys: bfloat16 [4096, 1024], P('context')
- context_values: bfloat16 [4096, 1024], P('context'), may hold values from -6 to 6
- query_span: int32 [2048], replicated, may hold values from 0 to 31
- query_position: int32 [2048], replicated, may hold values from 0 to 16383
- key_span: int32 [4096], replicated, may hold values from 0 to 31
- key_position: int32 [4096], replicated, may hold values from 0 to 16383
- tile_table: int32 [16, 32], replicated, may hold values 0 or 1
- residual: bfloat16 [2048, 7168], P('tensor', 'context')
- out_weight: bfloat16 [6144, 7168], P('tensor', 'context'), may hold values from -0.078125 to 0.078125
- norm_gain: bfloat16 [7168], P('context'), may hold values from 0.099609375 to 1.8984375
- gate_weight: bfloat16 [7168, 19200], P('context', 'tensor'), may hold values from -0.0625 to 0.0625
- up_weight: bfloat16 [7168, 19200], P('context', 'tensor'), may hold values from -0.0625 to 0.0625
- down_weight: bfloat16 [19200, 7168], P('tensor', 'context'), may hold values from -0.046875 to 0.046875
Outputs:
- attention: bfloat16 [2048, 6144], P('context', 'tensor')
- mixed: bfloat16 [2048, 7168], P('tensor', 'context')
All inputs are finite; a program needn't handle non-finite values.
Results may differ from a plain program's by a relative error of at most 0.022.
Values may be sent and summed in bfloat16 or wider, within the bound.
A program may use at most 128 MiB of HBM per device.

v0:
```python
import math

import jax
import jax.numpy as jnp
from jax import lax
from jax.sharding import PartitionSpec as P

D = 7168
HEADS = 48
KVH = 8
DH = 128
TILE = 128
SINK = 4


blocked_score = -1e30


def local(
    queries,
    context_keys,
    context_values,
    query_span,
    query_position,
    key_span,
    key_position,
    tile_table,
    residual,
    out_weight,
    norm_gain,
    gate_weight,
    up_weight,
    down_weight,
):
    context_place = lax.axis_index("context")
    tensor_place = lax.axis_index("tensor")
    query_rows = queries.shape[0]
    key_rows = context_keys.shape[0]
    heads_here = queries.shape[1] // DH
    grouped = HEADS // KVH
    query_tiles = tile_table.shape[0]
    key_tiles = tile_table.shape[1]
    table_float = tile_table.astype(jnp.float32)
    kv_head = tensor_place * heads_here // grouped
    keys_mine = lax.dynamic_slice_in_dim(context_keys, kv_head * DH, DH, 1)
    values_mine = lax.dynamic_slice_in_dim(context_values, kv_head * DH, DH, 1)
    own_first = context_place * query_rows

    def attend(query_heads, row_first, key_piece, value_piece, key_first, running):
        row_count = query_heads.shape[0]
        piece_rows = key_piece.shape[0]
        row_spans = lax.dynamic_slice_in_dim(query_span, row_first, row_count, 0)
        row_places = lax.dynamic_slice_in_dim(query_position, row_first, row_count, 0)
        row_tile = (row_first + jnp.arange(row_count, dtype=jnp.int32)) // TILE
        row_select = (
            row_tile[:, None] == jnp.arange(query_tiles, dtype=jnp.int32)[None, :]
        ).astype(jnp.float32)
        row_table = jnp.dot(row_select, table_float)
        key_index = key_first + jnp.arange(piece_rows, dtype=jnp.int32)
        column_select = (
            (key_index // TILE)[:, None] == jnp.arange(key_tiles, dtype=jnp.int32)[None, :]
        ).astype(jnp.float32)
        allowed = jnp.dot(row_table, column_select.T) > 0.5
        piece_spans = lax.dynamic_slice_in_dim(key_span, key_first, piece_rows, 0)
        piece_places = lax.dynamic_slice_in_dim(key_position, key_first, piece_rows, 0)
        visible = (key_index[None, :] < SINK) | allowed & (
            piece_spans[None, :] == row_spans[:, None]
        ) & (piece_places[None, :] < row_places[:, None])
        scores = jnp.einsum(
            "qhd,kd->hqk", query_heads, key_piece, preferred_element_type=jnp.float32
        ) / math.sqrt(DH)
        scores = jnp.where(visible[None], scores, blocked_score)
        old_max, old_total, old_sum = running
        new_max = jnp.maximum(old_max, jnp.max(scores, axis=2))
        factor = jnp.exp(old_max - new_max)
        weights = jnp.where(visible[None], jnp.exp(scores - new_max[:, :, None]), 0.0)
        new_total = old_total * factor + jnp.sum(weights, axis=2)
        new_sum = old_sum * factor[:, :, None] + jnp.einsum(
            "hqk,kd->hqd",
            weights.astype(jnp.bfloat16),
            value_piece,
            preferred_element_type=jnp.float32,
        )
        return (new_max, new_total, new_sum)

    own_heads = queries.reshape(query_rows, heads_here, DH)
    key_block = lax.all_gather(keys_mine, "context", axis=0, tiled=True)
    value_block = lax.all_gather(values_mine, "context", axis=0, tiled=True)
    piece_rows = key_block.shape[0]
    step_rows = math.gcd(piece_rows, key_rows)

    def one_step(step_number, state):
        begin = (step_number * step_rows).astype(jnp.int32)
        key_part = lax.dynamic_slice_in_dim(key_block, begin, step_rows, 0)
        value_part = lax.dynamic_slice_in_dim(value_block, begin, step_rows, 0)
        return attend(own_heads, own_first, key_part, value_part, begin, state)

    best_max, best_total, best_sum = lax.fori_loop(
        0,
        piece_rows // step_rows,
        one_step,
        (
            jnp.full((heads_here, query_rows), blocked_score, jnp.float32),
            jnp.zeros((heads_here, query_rows), jnp.float32),
            jnp.zeros((heads_here, query_rows, DH), jnp.float32),
        ),
    )
    attended = best_sum / best_total[:, :, None]
    attention = (
        attended.transpose(1, 0, 2).reshape(query_rows, heads_here * DH).astype(jnp.bfloat16)
    )
    all_heads = lax.all_gather(attention, "context", axis=0, tiled=True)
    projected = lax.psum_scatter(
        jnp.dot(all_heads, out_weight, preferred_element_type=jnp.float32).astype(jnp.bfloat16),
        "tensor",
        scatter_dimension=0,
        tiled=True,
    ).astype(jnp.float32)
    summed = (residual.astype(jnp.float32) + projected).astype(jnp.bfloat16)
    stream = summed.astype(jnp.float32)
    squares = lax.psum(jnp.sum(stream * stream, axis=1), "context")
    normed = (
        stream * lax.rsqrt(squares / D + 1e-05)[:, None] * norm_gain.astype(jnp.float32)
    ).astype(jnp.bfloat16)
    all_normed = lax.all_gather(normed, "tensor", axis=0, tiled=True)
    ff_here = gate_weight.shape[1]
    both_weights = jnp.concatenate([gate_weight, up_weight], axis=1)
    gate_up = lax.psum_scatter(
        jnp.dot(all_normed, both_weights, preferred_element_type=jnp.float32).astype(jnp.bfloat16),
        "context",
        scatter_dimension=0,
        tiled=True,
    ).astype(jnp.float32)
    hidden = (jax.nn.silu(gate_up[:, :ff_here]) * gate_up[:, ff_here:]).astype(jnp.bfloat16)
    all_hidden = lax.all_gather(hidden, "context", axis=0, tiled=True)
    down_sum = lax.psum_scatter(
        jnp.dot(all_hidden, down_weight, preferred_element_type=jnp.float32).astype(jnp.bfloat16),
        "tensor",
        scatter_dimension=0,
        tiled=True,
    ).astype(jnp.float32)
    mixed = (stream + down_sum).astype(jnp.bfloat16)
    return (attention, mixed)


def solution(mesh):
    placed = (
        P("context", "tensor"),
        P("context", None),
        P("context", None),
        P(),
        P(),
        P(),
        P(),
        P(),
        P("tensor", "context"),
        P("tensor", "context"),
        P("context"),
        P("context", "tensor"),
        P("context", "tensor"),
        P("tensor", "context"),
    )
    return jax.shard_map(
        local,
        mesh=mesh,
        in_specs=placed,
        out_specs=(P("context", "tensor"), P("tensor", "context")),
        check_vma=False,
    )
```

profile of v0, /device:TPU:16, one launch (start us, length us, event | category | flops | bytes accessed | tf_op | source)
XLA Modules:
  0.0 813.1 jit_solution(3513362289169395864)
XLA Ops:
  7.3 1.6 constant_dynamic-slice_fusion.1
  8.9 1.5 constant_dynamic-slice_fusion
  13.8 54.4 %all-gather.6.cloned.1.call-done = bf16[4096,128]{1,0:T(8,128)(2,1)} async-done(((bf16[256,128]{1,0:T(8,128)(2,1)}), bf16[4096,128]{1,0:T(8,128)(2,1)}) %all-gather.6.cloned.1.call-update) | async-done | bytes 1048592 | tf_op jit(solution)/shard_map/all_gather | solution.py:87
  68.2 54.6 %all-gather.8.cloned.1.call-done = bf16[4096,128]{1,0:T(8,128)(2,1)} async-done(((bf16[256,128]{1,0:T(8,128)(2,1)}), bf16[4096,128]{1,0:T(8,128)(2,1)}) %all-gather.8.cloned.1.call-update) | async-done | bytes 1048592 | tf_op jit(solution)/shard_map/all_gather | solution.py:88
  122.8 72.9 %while.21 = (s32[]{:T(128)}, f32[3,128]{1,0:T(4,128)S(1)}, f32[3,128]{1,0:T(4,128)S(1)}, f32[3,128,128]{2,1,0:T(8,128)S(1)}, s32[]{:T(128)}, /*index=5*/bf16[16,...) while((s32[]{:T(128)}, f32[3,128]{1,0:T(4,128)S(1)}, ...), condition=%wide.region_3.4_spmd.clone, body=%wide.region_0.3_spmd.clone.sunk | while | flops 53807492 | bytes 2035451 | solution.py:98
  126.2 1.2 convolution_add_fusion.2
  130.7 1.2 convolution_add_fusion.2
  135.3 1.2 convolution_add_fusion.2
  139.9 1.2 convolution_add_fusion.2
  144.4 1.2 convolution_add_fusion.2
  149.0 1.2 convolution_add_fusion.2
  153.5 1.2 convolution_add_fusion.2
  158.1 1.2 convolution_add_fusion.2
  162.6 1.2 convolution_add_fusion.2
  167.2 1.2 convolution_add_fusion.2
  176.3 1.2 convolution_add_fusion.2
  185.4 1.2 convolution_add_fusion.2
  194.5 1.2 convolution_add_fusion.2
  196.6 55.3 %all-gather.10.cloned.1.call-done = bf16[2048,384]{0,1:T(8,128)(2,1)} async-done(((bf16[128,384]{0,1:T(8,128)(2,1)}), bf16[2048,384]{0,1:T(8,128)(2,1)}) %all-gather.10.cloned.1.call-update) | async-done | bytes 1572880 | tf_op jit(solution)/shard_map/all_gather | solution.py:112
  251.9 2.5 convolution_convert_fusion.2
  254.4 2.4 copy.32
  257.5 85.1 %reduce-scatter.10.cloned.1.call-done = bf16[128,448]{1,0:T(8,128)(2,1)} async-done(((bf16[2048,448]{1,0:T(8,128)(2,1)}), bf16[128,448]{1,0:T(8,128)(2,1)}) %reduce-scatter.10.cloned.1.call-update) | async-done | bytes 114704
  343.8 37.9 %psum.7 = f32[128]{0:T(128)S(1)} all-reduce(f32[128]{0:T(128)S(1)} %fusion.29), channel_id=1, replica_groups=mesh['context'=16,'tensor'=16] {'context'}, use_global_device_ids=true, to_apply=%region_6.7 | all-reduce | flops 128 | bytes 1024 | tf_op jit(solution)/shard_map/psum | solution.py:121
  382.6 69.5 %all-gather.12.cloned.1.call-done = bf16[2048,448]{0,1:T(8,128)(2,1)} async-done(((bf16[128,448]{0,1:T(8,128)(2,1)}), bf16[2048,448]{0,1:T(8,128)(2,1)}) %all-gather.12.cloned.1.call-update) | async-done | bytes 1835024 | tf_op jit(solution)/shard_map/all_gather | solution.py:125
  452.0 10.5 %convolution_convert_fusion = bf16[2048,2400]{0,1:T(8,128)(2,1)} fusion(bf16[2048,448]{0,1:T(8,128)(2,1)} %all-gather.12.cloned.1.call-done, bf16[448,1200]{1,0:T(8,128)(2,1)S(1)} %copy-done.5, bf16[448,1200]{1,0:T(8,128)(2,1)} %param.27), kind=kOutput, calls=%fused_computation.41 | convolution fusion | flops 4413235200 | bytes 13815808 | tf_op jit(solution)/shard_map/dot_general | solution.py:129
  462.5 13.3 %copy.34 = bf16[2048,2400]{1,0:T(8,128)(2,1)} copy(bf16[2048,2400]{0,1:T(8,128)(2,1)} %convolution_convert_fusion) | data formatting | bytes 19660800
  476.0 153.4 %reduce-scatter.12.cloned.1.call-done = bf16[128,2400]{1,0:T(8,128)(2,1)} async-done(((bf16[2048,2400]{1,0:T(8,128)(2,1)}), bf16[128,2400]{1,0:T(8,128)(2,1)}) %reduce-scatter.12.cloned.1.call-update) | async-done | bytes 614416
  629.3 1.4 copy.35
  631.8 79.8 %all-gather.14.cloned.1.call-done = bf16[2048,1200]{0,1:T(8,128)(2,1)} async-done(((bf16[128,1200]{0,1:T(8,128)(2,1)}), bf16[2048,1200]{0,1:T(8,128)(2,1)}) %all-gather.14.cloned.1.call-update) | async-done | bytes 4915216 | tf_op jit(solution)/shard_map/all_gather | solution.py:135
  711.6 4.9 convolution_convert_fusion.1
  716.5 2.4 copy.36
  720.6 83.9 %reduce-scatter.14.cloned.1.call-done = bf16[128,448]{1,0:T(8,128)(2,1)} async-done(((bf16[2048,448]{1,0:T(8,128)(2,1)}), bf16[128,448]{1,0:T(8,128)(2,1)}) %reduce-scatter.14.cloned.1.call-update) | async-done | bytes 114704
  (243 shorter events, 67.8 us)
Async XLA Ops:
  7.2 704.4 %copy-start = (bf16[1200,448]{0,1:T(8,128)(2,1)S(1)}, bf16[1200,448]{0,1:T(8,128)(2,1)}, u32[]{:S(2)}) copy-start(bf16[1200,448]{0,1:T(8,128)(2,1)} %param.29) | copy-start | bytes 3225604
  7.2 61.0 %all-gather.6.cloned.1.call-start = ((), (), s32[]{:S(2)}) async-start(), calls=%async_computation.3 | async-start | bytes 1114112 | tf_op jit(solution)/shard_map/all_gather | solution.py:87
  8.8 114.0 %all-gather.8.cloned.1.call-start = ((), (), s32[]{:S(2)}) async-start(), calls=%async_computation.4 | async-start | bytes 1114112 | tf_op jit(solution)/shard_map/all_gather | solution.py:88
  10.4 241.5 %all-gather.10.cloned.1.call-start = ((), (), s32[]{:S(2)}) async-start(), calls=%async_computation.5 | async-start | bytes 1671168 | tf_op jit(solution)/shard_map/all_gather | solution.py:112
  122.8 129.1 %copy-start.3 = (bf16[384,448]{0,1:T(8,128)(2,1)S(1)}, bf16[384,448]{0,1:T(8,128)(2,1)}, u32[]{:S(2)}) copy-start(bf16[384,448]{0,1:T(8,128)(2,1)} %param.25) | copy-start | bytes 1032196
  196.5 146.1 %reduce-scatter.10.cloned.1.call-start = ((), (), s32[]{:S(2)}) async-start(), calls=%async_computation.8 | async-start | bytes 2228224
  256.8 0.7 copy-start.4
  256.8 86.8 %copy-start.1 = (bf16[128,448]{0,1:T(8,128)(2,1)S(1)}, bf16[128,448]{0,1:T(8,128)(2,1)}, u32[]{:S(2)}) copy-start(bf16[128,448]{0,1:T(8,128)(2,1)} %param.24) | copy-start | bytes 344068
  256.8 195.2 %copy-start.5 = (bf16[448,1200]{1,0:T(8,128)(2,1)S(1)}, bf16[448,1200]{1,0:T(8,128)(2,1)}, u32[]{:S(2)}) copy-start(bf16[448,1200]{1,0:T(8,128)(2,1)} %param.28) | copy-start | bytes 3225604
  256.9 195.2 %all-gather.12.cloned.1.call-start = ((), (), s32[]{:S(2)}) async-start(), calls=%async_computation.6 | async-start | bytes 1949696 | tf_op jit(solution)/shard_map/all_gather | solution.py:125
  382.5 246.8 %reduce-scatter.12.cloned.1.call-start = ((), (), s32[]{:S(2)}) async-start(), calls=%async_computation.9 | async-start | bytes 10584064
  475.9 235.7 %all-gather.14.cloned.1.call-start = ((), (), s32[]{:S(2)}) async-start(), calls=%async_computation.7 | async-start | bytes 5222400 | tf_op jit(solution)/shard_map/all_gather | solution.py:135
  631.7 172.8 %reduce-scatter.14.cloned.1.call-start = ((), (), s32[]{:S(2)}) async-start(), calls=%async_computation.10 | async-start | bytes 2228224
  719.0 0.9 copy-start.2
Sparse Core Ops, SparseCore 0:
  11.3 56.8 all-gather.5
  71.5 51.2 all-gather.7
  196.7 55.1 all-gather.9
  257.0 85.6 reduce-scatter.9
  382.6 69.3 all-gather.11
  476.0 153.2 reduce-scatter.11
  632.2 79.3 all-gather.13
  719.1 85.3 reduce-scatter.13
where the time goes:
time: 816 us; the launch traced here: 813 us
  waiting for transfers between devices  636 us (78%)
  matrix products  60.8 us (7%)
  local copies, waits for them, and re-layouts  56.2 us (7%)
  blocking collectives  37.9 us (5%)
  between operations  14.3 us (2%)
    unnamed x11, waiting for transfers between devices  323 us
    all_gather x1, waiting for transfers between devices, local(): all_hidden = lax.all_gather(hidden, 'context', axis=0, tiled=True)  79.8 us
    all_gather x1, waiting for transfers between devices, local(): all_normed = lax.all_gather(normed, 'tensor', axis=0, tiled=True)  69.5 us
    all_gather x1, waiting for transfers between devices, local(): all_heads = lax.all_gather(attention, 'context', axis=0, tiled=True)  55.3 us
    all_gather x1, waiting for transfers between devices, local(): value_block = lax.all_gather(values_mine, 'context', axis=0, tiled=True)  54.6 us
    all_gather x1, waiting for transfers between devices, local(): key_block = lax.all_gather(keys_mine, 'context', axis=0, tiled=True)  54.4 us
    psum x1, blocking collectives, local(): squares = lax.psum(jnp.sum(stream * stream, axis=1), 'context')  37.9 us
    unnamed x21, local copies, waits for them, and re-layouts  25.1 us
  transfers between devices with their start and end apart: 8, of which 8 were waited for; matrix products, arithmetic and copies ran while one was open for 1% of the time, Pallas kernels for 0%

commit v1 on v0

v1 whole, which is shorter than its diff:
```python
import math

import jax
import jax.numpy as jnp
from jax import lax
from jax.experimental import pallas as pl
from jax.experimental.pallas import tpu as pltpu
from jax.sharding import PartitionSpec as P

MESH = pl.DeviceIdType.MESH
F32 = jnp.float32
BF16 = jnp.bfloat16

D = 7168
DH = 128
TILE = 128
SINK = 4
ROWS = 128
HALF = ROWS // 2
NH = 3
KROWS = 256
COLS = 448
CC = 2 * COLS
FF = 1200
BLOCKS = 8

BLOCKED = -1e30
SCORE_SCALE = math.log2(math.e) / math.sqrt(DH)

N_COPIES = 140


def layer_kernel(
    q_ref,
    key_ref,
    value_ref,
    qspan_ref,
    qpos_ref,
    kspan_ref,
    kpos_ref,
    table_ref,
    res_ref,
    wo_ref,
    gain_ref,
    wg_ref,
    wu_ref,
    wd_ref,
    att_out,
    mix_out,
    kv,
    q3,
    m_s,
    l_s,
    acc_s,
    att,
    wo_in,
    wo2,
    wd_in,
    wd2,
    wg2,
    wu2,
    res2,
    gain2,
    part,
    half_in,
    full_in,
    z_out,
    z_in,
    stream,
    sq_out,
    sq_in,
    normed,
    gu,
    gu_half,
    gu_full,
    gu_z,
    hid,
    part2,
    half_in2,
    full_in2,
    z_out2,
    z_in2,
    mix_send,
    mix_recv,
    send_sem,
    recv_sem,
    local_sem,
):
    c = lax.axis_index("context")
    t = lax.axis_index("tensor")
    y, z, k = c // 4, lax.rem(c // 2, 2), lax.rem(c, 2)
    zl, x = t // 4, lax.rem(t, 4)
    yp, ym, yo = lax.rem(y + 1, 4), lax.rem(y + 3, 4), lax.rem(y + 2, 4)
    xp, xm = lax.rem(x + 1, 4), lax.rem(x + 3, 4)
    zo, ko = 1 - z, 1 - k

    def dev(y_=None, z_=None, k_=None, zl_=None, x_=None):
        y_ = y if y_ is None else y_
        z_ = z if z_ is None else z_
        k_ = k if k_ is None else k_
        zl_ = zl if zl_ is None else zl_
        x_ = x if x_ is None else x_
        return (4 * y_ + 2 * z_ + k_, 4 * zl_ + x_)

    sibling, across = dev(k_=ko), dev(z_=zo)
    up_y, down_y = dev(y_=yp), dev(y_=ym)
    up_x, down_x = dev(x_=xp), dev(x_=xm)
    zl_peers = [dev(zl_=lax.rem(zl + d, 4)) for d in (1, 2, 3)]
    norm_peers = [
        dev(y_=lax.rem(y + dy, 4), z_=lax.rem(z + dz, 2))
        for dy in range(4)
        for dz in range(2)
        if dy or dz
    ]
    is_home = lax.rem(x + k, 2) == 0
    is_relay = lax.rem(x + k, 2) == 1

    count = [0]
    sent = []

    def new_id():
        count[0] += 1
        return count[0] - 1

    def copy(src, dst, to, number):
        return pltpu.make_async_remote_copy(
            src_ref=src,
            dst_ref=dst,
            send_sem=send_sem.at[number],
            recv_sem=recv_sem.at[number],
            device_id=to,
            device_id_type=MESH,
        )

    def send(src, dst, to, number):
        one = copy(src, dst, to, number)
        one.start()
        sent.append(one)

    def arrived(dst, number):
        copy(dst, dst, sibling, number).wait_recv()

    kv_head = t // 2
    head_columns = pl.ds(pl.multiple_of(kv_head * DH, DH), DH)
    loads = [
        pltpu.make_async_copy(key_ref.at[:, head_columns], kv.at[c, :, 0:DH], local_sem.at[0]),
        pltpu.make_async_copy(
            value_ref.at[:, head_columns], kv.at[c, :, DH : 2 * DH], local_sem.at[1]
        ),
        pltpu.make_async_copy(wo_ref, wo_in.at[k], local_sem.at[2]),
        pltpu.make_async_copy(res_ref, res2.at[k], local_sem.at[3]),
        pltpu.make_async_copy(gain_ref, gain2.at[k], local_sem.at[4]),
        pltpu.make_async_copy(
            wg_ref, wg2.at[pl.ds(pl.multiple_of(k * COLS, COLS), COLS)], local_sem.at[5]
        ),
        pltpu.make_async_copy(
            wu_ref, wu2.at[pl.ds(pl.multiple_of(k * COLS, COLS), COLS)], local_sem.at[6]
        ),
        pltpu.make_async_copy(wd_ref, wd_in.at[k], local_sem.at[7]),
    ]
    for one in loads:
        one.start()

    barrier = pltpu.get_barrier_semaphore()
    peers = [sibling, up_x, down_x] + zl_peers + norm_peers
    for peer in peers:
        pl.semaphore_signal(barrier, inc=1, device_id=peer, device_id_type=MESH)
    pl.semaphore_wait(barrier, len(peers))

    loads[0].wait()
    loads[1].wait()
    ids = [new_id() for _ in range(17)]

    def block_at(y_, z_, k_):
        return kv.at[4 * y_ + 2 * z_ + k_]

    def half_at(y_, z_, k_, h):
        return kv.at[4 * y_ + 2 * z_ + k_, h * (KROWS // 2) : (h + 1) * (KROWS // 2)]

    own = block_at(y, z, k)
    send(own, own, across, ids[0])
    send(own, own, up_y, ids[1])
    send(own, own, down_y, ids[2])
    send(own, own, sibling, ids[3])

    for one in loads[2:]:
        one.wait()
    weight_ids = [new_id() for _ in range(6)]
    half_rows = pl.ds(pl.multiple_of(k * COLS, COLS), COLS)
    other_rows = pl.ds(pl.multiple_of(ko * COLS, COLS), COLS)

    other = block_at(y, zo, k)
    arrived(other, ids[0])
    send(other, other, up_y, ids[4])
    send(other, other, down_y, ids[5])
    send(other, other, sibling, ids[6])
    b = block_at(ym, z, k)
    arrived(b, ids[1])
    send(half_at(ym, z, k, 0), half_at(ym, z, k, 0), up_y, ids[7])
    send(b, b, sibling, ids[9])
    b = block_at(yp, z, k)
    arrived(b, ids[2])
    send(half_at(yp, z, k, 1), half_at(yp, z, k, 1), down_y, ids[8])
    send(b, b, sibling, ids[10])
    b = block_at(ym, zo, k)
    arrived(b, ids[4])
    send(half_at(ym, zo, k, 0), half_at(ym, zo, k, 0), up_y, ids[11])
    send(b, b, sibling, ids[13])
    b = block_at(yp, zo, k)
    arrived(b, ids[5])
    send(half_at(yp, zo, k, 1), half_at(yp, zo, k, 1), down_y, ids[12])
    send(b, b, sibling, ids[14])

    for h in range(NH):
        q3[h] = q_ref[:, h * DH : (h + 1) * DH]
    m_s[...] = jnp.full(m_s.shape, BLOCKED, F32)
    l_s[...] = jnp.zeros(l_s.shape, F32)
    acc_s[...] = jnp.zeros(acc_s.shape, F32)

    def as_column(row):
        return jnp.broadcast_to(row.astype(F32), (ROWS, ROWS)).T.astype(jnp.int32)

    q_span = as_column(qspan_ref[pl.ds(c, 1), :])
    q_pos = as_column(qpos_ref[pl.ds(c, 1), :])

    def attend(group):
        visible = []
        for n in range(8):
            tile = 8 * group + n
            allowed = table_ref[c, tile] == 1
            spans = jnp.where(allowed, kspan_ref[pl.ds(tile, 1), :], -1)
            places = kpos_ref[pl.ds(tile, 1), :]
            index = tile * TILE + lax.broadcasted_iota(jnp.int32, (1, TILE), 1)
            spans = jnp.broadcast_to(spans, (ROWS, TILE))
            places = jnp.broadcast_to(places, (ROWS, TILE))
            index = jnp.broadcast_to(index, (ROWS, TILE))
            visible.append(
                jnp.where(
                    ((spans == q_span) & (places < q_pos)) | (index < SINK), 0.0, BLOCKED
                ).astype(F32)
            )
        keys = kv[pl.ds(4 * group, 4)].reshape(4 * KROWS, 2 * DH)

        def one_head(h, carry):
            scores = lax.dot_general(
                q3[h], keys[:, :DH], (((1,), (1,)), ((), ())), preferred_element_type=F32
            )
            pieces = [
                jnp.where(
                    visible[n] == 0.0,
                    scores[:, n * TILE : (n + 1) * TILE] * SCORE_SCALE,
                    BLOCKED,
                )
                for n in range(8)
            ]
            best = pieces[0]
            for piece in pieces[1:]:
                best = jnp.maximum(best, piece)
            old = m_s[h]
            new = jnp.maximum(old, jnp.max(best, axis=1, keepdims=True))
            factor = jnp.exp2(old - new)
            weights = [jnp.exp2(piece - new) for piece in pieces]
            total = weights[0]
            for one in weights[1:]:
                total = total + one
            m_s[h] = new
            l_s[h] = l_s[h] * factor + total
            rounded = jnp.concatenate([one.astype(BF16) for one in weights], axis=1)
            acc_s[h] = acc_s[h] * factor + jnp.dot(
                rounded, keys[:, DH:], preferred_element_type=F32
            )
            return carry

        lax.fori_loop(0, NH, one_head, 0)

    arrived(block_at(y, z, ko), ids[3])
    arrived(block_at(y, zo, ko), ids[6])
    attend(y)

    arrived(half_at(yo, z, k, 0), ids[7])
    arrived(half_at(yo, z, k, 1), ids[8])
    b = block_at(yo, z, k)
    send(b, b, sibling, ids[15])
    arrived(half_at(yo, zo, k, 0), ids[11])
    arrived(half_at(yo, zo, k, 1), ids[12])
    b = block_at(yo, zo, k)
    send(b, b, sibling, ids[16])

    arrived(block_at(ym, z, ko), ids[9])
    arrived(block_at(ym, zo, ko), ids[13])
    attend(ym)
    arrived(block_at(yp, z, ko), ids[10])
    arrived(block_at(yp, zo, ko), ids[14])
    attend(yp)
    arrived(block_at(yo, z, ko), ids[15])
    arrived(block_at(yo, zo, ko), ids[16])
    attend(yo)

    mine = 2 * y + z
    for h in range(NH):
        total = jnp.sum(l_s[h], axis=1, keepdims=True)
        att[mine, :, h * DH : (h + 1) * DH] = (acc_s[h] / total).astype(BF16)

    def gather_context(buf, ready):
        ids = [new_id() for _ in range(9)]

        def whole(y_, z_):
            return buf.at[2 * y_ + z_]

        def part_of(y_, z_, h):
            return buf.at[2 * y_ + z_, h * HALF : (h + 1) * HALF]

        own = whole(y, z)
        send(own, own, across, ids[0])
        send(own, own, up_y, ids[1])
        send(own, own, down_y, ids[2])
        ready(2 * y + z)
        b = whole(y, zo)
        arrived(b, ids[0])
        send(b, b, up_y, ids[3])
        send(b, b, down_y, ids[4])
        arrived(whole(ym, z), ids[1])
        send(part_of(ym, z, 0), part_of(ym, z, 0), up_y, ids[5])
        arrived(whole(yp, z), ids[2])
        send(part_of(yp, z, 1), part_of(yp, z, 1), down_y, ids[6])
        ready(2 * y + zo)
        ready(2 * ym + z)
        ready(2 * yp + z)
        arrived(whole(ym, zo), ids[3])
        send(part_of(ym, zo, 0), part_of(ym, zo, 0), up_y, ids[7])
        arrived(whole(yp, zo), ids[4])
        send(part_of(yp, zo, 1), part_of(yp, zo, 1), down_y, ids[8])
        ready(2 * ym + zo)
        ready(2 * yp + zo)
        arrived(part_of(yo, z, 0), ids[5])
        arrived(part_of(yo, z, 1), ids[6])
        ready(2 * yo + z)
        arrived(part_of(yo, zo, 0), ids[7])
        arrived(part_of(yo, zo, 1), ids[8])
        ready(2 * yo + zo)

    send(wo_in.at[k], wo_in.at[k], sibling, weight_ids[0])
    send(res2.at[k], res2.at[k], sibling, weight_ids[1])
    send(gain2.at[k], gain2.at[k], sibling, weight_ids[2])
    send(wg2.at[half_rows], wg2.at[half_rows], sibling, weight_ids[3])
    send(wu2.at[half_rows], wu2.at[half_rows], sibling, weight_ids[4])
    send(wd_in.at[k], wd_in.at[k], sibling, weight_ids[5])

    first = [True]

    def project(i):
        if first[0]:
            first[0] = False
            arrived(wo_in.at[ko], weight_ids[0])
            wo2[...] = jnp.concatenate([wo_in[0], wo_in[1]], axis=1)
        part[i] = jnp.dot(att[i], wo2[...], preferred_element_type=F32).astype(BF16)

    gather_context(att, project)
    att_out[...] = att[mine]

    home_j = x // 2
    plus_j, minus_j = xp // 2, xm // 2

    def scatter_tensor(shares, halves, fulls, out, inn, finish):
        half_ids = [[new_id() for _ in range(2)] for _ in range(4)]
        full_ids = [[new_id() for _ in range(2)] for _ in range(4)]
        z_ids = [new_id() for _ in range(3)]
        order = [(d, lax.rem(zl + d, 4)) for d in (2, 1, 3, 0)]

        @pl.when(is_home)
        def _():
            kept = list(sent)
            sent.clear()
            for d, to in order:
                i = 2 * to + 1 - home_j
                send(shares.at[i, 0:HALF], halves.at[0, to], up_x, half_ids[d][0])
                send(shares.at[i, HALF:ROWS], halves.at[1, to], down_x, half_ids[d][1])
            total = None
            for d, to in order:
                arrived(fulls.at[0, to], full_ids[d][0])
                arrived(fulls.at[1, to], full_ids[d][1])
                here = (
                    shares[2 * to + home_j].astype(F32)
                    + fulls[0, to].astype(F32)
                    + fulls[1, to].astype(F32)
                )
                if d:
                    out[d - 1] = here.astype(BF16)
                    send(out.at[d - 1], inn.at[d - 1], zl_peers[d - 1], z_ids[d - 1])
                else:
                    total = here
            for d in (1, 3, 2):
                arrived(inn.at[d - 1], z_ids[d - 1])
                total = total + inn[d - 1].astype(F32)
            finish(total)
            for one in sent:
                one.wait_send()
            sent.clear()
            sent.extend(kept)

        @pl.when(is_relay)
        def _():
            kept = list(sent)
            sent.clear()
            for d, to in order:
                i = 2 * to + plus_j
                arrived(halves.at[0, to], half_ids[d][0])
                shares[i, 0:HALF] = (
                    shares[i, 0:HALF].astype(F32) + halves[0, to].astype(F32)
                ).astype(BF16)
                send(shares.at[i], fulls.at[0, to], up_x, full_ids[d][0])
                i = 2 * to + minus_j
                arrived(halves.at[1, to], half_ids[d][1])
                shares[i, HALF:ROWS] = (
                    shares[i, HALF:ROWS].astype(F32) + halves[1, to].astype(F32)
                ).astype(BF16)
                send(shares.at[i], fulls.at[1, to], down_x, full_ids[d][1])
            for one in sent:
                one.wait_send()
            sent.clear()
            sent.extend(kept)

    arrived(res2.at[ko], weight_ids[1])
    arrived(gain2.at[ko], weight_ids[2])
    norm_ids = [new_id() for _ in range(7)]
    gather_z = [new_id() for _ in range(3)]
    gather_x = [[new_id() for _ in range(2)] for _ in range(4)]
    gather_half = [[new_id() for _ in range(2)] for _ in range(4)]

    def normalise(total):
        res = jnp.concatenate([res2[0].astype(F32), res2[1].astype(F32)], axis=1)
        rounded = (res + total).astype(BF16)
        stream[...] = rounded
        st = rounded.astype(F32)
        squares = jnp.sum(st * st, axis=1, keepdims=True)
        sq_out[...] = jnp.broadcast_to(squares, (ROWS, ROWS)).T[0:8]
        for n, peer in enumerate(norm_peers):
            send(sq_out, sq_in.at[n], peer, norm_ids[n])
        whole = sq_out[...]
        for n in range(7):
            arrived(sq_in.at[n], norm_ids[n])
            whole = whole + sq_in[n]
        column = jnp.broadcast_to(whole[0:1], (ROWS, ROWS)).T[:, 0:1]
        gain = jnp.concatenate([gain2[0][0:1], gain2[1][0:1]], axis=1)
        i = 2 * zl + home_j
        normed[i] = (st * lax.rsqrt(column / D + 1e-05) * gain).astype(BF16)
        own = normed.at[i]
        for d in (1, 2, 3):
            send(own, own, zl_peers[d - 1], gather_z[d - 1])
        for d in (0, 1, 3, 2):
            b = normed.at[2 * lax.rem(zl + 4 - d, 4) + home_j]
            if d:
                arrived(b, gather_z[d - 1])
            send(b, b, up_x, gather_x[d][0])
            send(b, b, down_x, gather_x[d][1])
        for d in (0, 1, 3, 2):
            i = 2 * lax.rem(zl + 4 - d, 4) + 1 - home_j
            arrived(normed.at[i, 0:HALF], gather_half[d][0])
            arrived(normed.at[i, HALF:ROWS], gather_half[d][1])

    scatter_tensor(part, half_in, full_in, z_out, z_in, normalise)

    @pl.when(is_relay)
    def _():
        kept = list(sent)
        sent.clear()
        for d in (0, 1, 3, 2):
            i = 2 * lax.rem(zl + 4 - d, 4) + minus_j
            arrived(normed.at[i], gather_x[d][0])
            send(normed.at[i, 0:HALF], normed.at[i, 0:HALF], up_x, gather_half[d][0])
            i = 2 * lax.rem(zl + 4 - d, 4) + plus_j
            arrived(normed.at[i], gather_x[d][1])
            send(normed.at[i, HALF:ROWS], normed.at[i, HALF:ROWS], down_x, gather_half[d][1])
        for one in sent:
            one.wait_send()
        sent.clear()
        sent.extend(kept)

    arrived(wg2.at[other_rows], weight_ids[3])
    arrived(wu2.at[other_rows], weight_ids[4])

    def gate_up(i):
        rows = normed[i]
        gu[i, 0] = jnp.dot(rows, wg2[...], preferred_element_type=F32).astype(BF16)
        gu[i, 1] = jnp.dot(rows, wu2[...], preferred_element_type=F32).astype(BF16)

    first_ids = [[new_id() for _ in range(2)] for _ in range(2)]
    second_ids = [[new_id() for _ in range(2)] for _ in range(2)]
    cross_id = new_id()
    z_order = [(0, zo), (1, z)]

    def far(n, carry):
        gate_up(2 * yo + lax.rem(z + 1 + n, 2))
        return carry

    def near(n, carry):
        gate_up(2 * lax.rem(y + 1 + 2 * lax.rem(n, 2), 4) + lax.rem(z + 1 + n // 2, 2))
        return carry

    def own_rows(n, carry):
        gate_up(2 * y + lax.rem(z + 1 + n, 2))
        return carry

    lax.fori_loop(0, 2, far, 0)
    for n, zz in z_order:
        i = 2 * yo + zz
        send(gu.at[i, :, 0:HALF], gu_half.at[0, n], up_y, first_ids[n][0])
        send(gu.at[i, :, HALF:ROWS], gu_half.at[1, n], down_y, first_ids[n][1])
    lax.fori_loop(0, 4, near, 0)
    for n, zz in z_order:
        i = 2 * yp + zz
        arrived(gu_half.at[0, n], first_ids[n][0])
        gu[i, :, 0:HALF] = (gu[i, :, 0:HALF].astype(F32) + gu_half[0, n].astype(F32)).astype(BF16)
        send(gu.at[i], gu_full.at[0, n], up_y, second_ids[n][0])
        i = 2 * ym + zz
        arrived(gu_half.at[1, n], first_ids[n][1])
        gu[i, :, HALF:ROWS] = (
            gu[i, :, HALF:ROWS].astype(F32) + gu_half[1, n].astype(F32)
        ).astype(BF16)
        send(gu.at[i], gu_full.at[1, n], down_y, second_ids[n][1])
    lax.fori_loop(0, 2, own_rows, 0)
    arrived(wd_in.at[ko], weight_ids[5])
    wd2[...] = jnp.concatenate([wd_in[0], wd_in[1]], axis=1)

    def own_sum(n, zz, which):
        return (
            gu[2 * y + zz, which].astype(F32)
            + gu_full[0, n, which].astype(F32)
            + gu_full[1, n, which].astype(F32)
        )

    arrived(gu_full.at[0, 0], second_ids[0][0])
    arrived(gu_full.at[1, 0], second_ids[0][1])
    gu[2 * y + zo, 0] = own_sum(0, zo, 0).astype(BF16)
    gu[2 * y + zo, 1] = own_sum(0, zo, 1).astype(BF16)
    send(gu.at[2 * y + zo], gu_z, across, cross_id)
    arrived(gu_full.at[0, 1], second_ids[1][0])
    arrived(gu_full.at[1, 1], second_ids[1][1])
    arrived(gu_z, cross_id)
    gate = own_sum(1, z, 0) + gu_z[0].astype(F32)
    up = own_sum(1, z, 1) + gu_z[1].astype(F32)
    hid[mine] = (gate / (1.0 + jnp.exp(-gate)) * up).astype(BF16)

    def down(i):
        part2[i] = jnp.dot(hid[i], wd2[...], preferred_element_type=F32).astype(BF16)

    gather_context(hid, down)

    mix_id = new_id()

    def mix(total):
        mixed = stream[...].astype(F32) + total
        low, high = mixed[:, :COLS], mixed[:, COLS:]
        mix_out[...] = jnp.where(k == 0, low, high).astype(BF16)
        mix_send[...] = jnp.where(k == 0, high, low).astype(BF16)
        send(mix_send, mix_recv, sibling, mix_id)

    scatter_tensor(part2, half_in2, full_in2, z_out2, z_in2, mix)

    @pl.when(is_relay)
    def _():
        arrived(mix_recv, mix_id)
        mix_out[...] = mix_recv[...]

    for one in sent:
        one.wait_send()
    assert count[0] <= N_COPIES


def local(
    queries,
    context_keys,
    context_values,
    query_span,
    query_position,
    key_span,
    key_position,
    tile_table,
    residual,
    out_weight,
    norm_gain,
    gate_weight,
    up_weight,
    down_weight,
):
    vmem = pl.BlockSpec(memory_space=pltpu.VMEM)
    smem = pl.BlockSpec(memory_space=pltpu.SMEM)
    hbm = pl.BlockSpec(memory_space=pl.ANY)
    gain = jnp.broadcast_to(norm_gain.astype(F32)[None, :], (8, COLS))
    scratch = [
        pltpu.VMEM((16, KROWS, 2 * DH), BF16),
        pltpu.VMEM((NH, ROWS, DH), BF16),
        pltpu.VMEM((NH, ROWS, DH), F32),
        pltpu.VMEM((NH, ROWS, DH), F32),
        pltpu.VMEM((NH, ROWS, DH), F32),
        pltpu.VMEM((BLOCKS, ROWS, NH * DH), BF16),
        pltpu.VMEM((2, NH * DH, COLS), BF16),
        pltpu.VMEM((NH * DH, CC), BF16),
        pltpu.VMEM((2, FF, COLS), BF16),
        pltpu.VMEM((FF, CC), BF16),
        pltpu.VMEM((CC, FF), BF16),
        pltpu.VMEM((CC, FF), BF16),
        pltpu.VMEM((2, ROWS, COLS), BF16),
        pltpu.VMEM((2, 8, COLS), F32),
        pltpu.VMEM((BLOCKS, ROWS, CC), BF16),
        pltpu.VMEM((2, 4, HALF, CC), BF16),
        pltpu.VMEM((2, 4, ROWS, CC), BF16),
        pltpu.VMEM((3, ROWS, CC), BF16),
        pltpu.VMEM((3, ROWS, CC), BF16),
        pltpu.VMEM((ROWS, CC), BF16),
        pltpu.VMEM((8, ROWS), F32),
        pltpu.VMEM((7, 8, ROWS), F32),
        pltpu.VMEM((BLOCKS, ROWS, CC), BF16),
        pltpu.VMEM((BLOCKS, 2, ROWS, FF), BF16),
        pltpu.VMEM((2, 2, 2, HALF, FF), BF16),
        pltpu.VMEM((2, 2, 2, ROWS, FF), BF16),
        pltpu.VMEM((2, ROWS, FF), BF16),
        pltpu.VMEM((BLOCKS, ROWS, FF), BF16),
        pltpu.VMEM((BLOCKS, ROWS, CC), BF16),
        pltpu.VMEM((2, 4, HALF, CC), BF16),
        pltpu.VMEM((2, 4, ROWS, CC), BF16),
        pltpu.VMEM((3, ROWS, CC), BF16),
        pltpu.VMEM((3, ROWS, CC), BF16),
        pltpu.VMEM((ROWS, COLS), BF16),
        pltpu.VMEM((ROWS, COLS), BF16),
        pltpu.SemaphoreType.DMA((N_COPIES,)),
        pltpu.SemaphoreType.DMA((N_COPIES,)),
        pltpu.SemaphoreType.DMA((8,)),
    ]
    return pl.pallas_call(
        layer_kernel,
        out_shape=(
            jax.ShapeDtypeStruct(queries.shape, BF16),
            jax.ShapeDtypeStruct(residual.shape, BF16),
        ),
        in_specs=[vmem, hbm, hbm, vmem, vmem, vmem, vmem, smem, hbm, hbm, hbm, hbm, hbm, hbm],
        out_specs=(vmem, vmem),
        scratch_shapes=scratch,
        compiler_params=pltpu.CompilerParams(
            collective_id=0, has_side_effects=True, vmem_limit_bytes=60 * 2**20
        ),
        cost_estimate=pl.CostEstimate(
            flops=9_000_000_000, bytes_accessed=8_000_000, transcendentals=2_000_000
        ),
        name="layer",
    )(
        queries,
        context_keys,
        context_values,
        query_span.reshape(16, TILE),
        query_position.reshape(16, TILE),
        key_span.reshape(32, TILE),
        key_position.reshape(32, TILE),
        tile_table,
        residual,
        out_weight,
        gain,
        gate_weight,
        up_weight,
        down_weight,
    )


def solution(mesh):
    placed = (
        P("context", "tensor"),
        P("context", None),
        P("context", None),
        P(),
        P(),
        P(),
        P(),
        P(),
        P("tensor", "context"),
        P("tensor", "context"),
        P("context"),
        P("context", "tensor"),
        P("context", "tensor"),
        P("tensor", "context"),
    )
    return jax.shard_map(
        local,
        mesh=mesh,
        in_specs=placed,
        out_specs=(P("context", "tensor"), P("tensor", "context")),
        check_vma=False,
    )
```

time: 816 us -> 228 us (0.28)
  waiting for transfers between devices: 636 us -> 0 us
  Pallas kernels: 0 us -> 213 us
  matrix products: 60.8 us -> 0 us
  local copies, waits for them, and re-layouts: 56.2 us -> 10.4 us
  blocking collectives: 37.9 us -> 0 us
  between operations: 14.3 us -> 0.64 us
    unnamed x11 -> x0, waiting for transfers between devices: 323 us -> none
    all_gather x5 -> x0, waiting for transfers between devices: 314 us -> none  [the longest x1 79.8 us: local(): all_hidden = lax.all_gather(hidden, 'context', axis=0, tiled=True)]
    pallas_call x0 -> x1, Pallas kernels: none -> 213 us  [local(): pl.pallas_call(layer_kernel, out_shape=(jax.ShapeDtypeStruct(queries.shap...]
    dot_general x51 -> x0, matrix products: 60.8 us -> none  [the longest x16 18.7 us: attend(): jnp.einsum('hqk,kd->hqd', weights.astype(jnp.bfloat16), value_piece, pref...]
    psum x1 -> x0, blocking collectives: 37.9 us -> none  [local(): squares = lax.psum(jnp.sum(stream * stream, axis=1), 'context')]
    dynamic_slice x36 -> x0, local copies, waits for them, and re-layouts: 29 us -> none  [the longest x16 12.3 us: attend(): lax.dynamic_slice_in_dim(key_position, key_first, piece_rows, 0)]
    unnamed x21 -> x4, local copies, waits for them, and re-layouts: 25.1 us -> 7.49 us
  transfers between devices with their start and end apart: 8 -> 0, of which waited for: 8 -> 0; matrix products, arithmetic and copies ran while one was open for 1% -> 0% of each run, Pallas kernels for 0% -> 0%
where the time goes in v1:
time: 228 us; the launch traced here: 224 us
  Pallas kernels  213 us (93%)
  local copies, waits for them, and re-layouts  10.4 us (5%)
    pallas_call x1, Pallas kernels, local(): pl.pallas_call(layer_kernel, out_shape=(jax.ShapeDtypeStruct(queries.shap...  213 us
    unnamed x4, local copies, waits for them, and re-layouts  7.49 us

profile of v1, /device:TPU:16, one launch (start us, length us, event | category | flops | bytes accessed | tf_op | source)
XLA Modules:
  0.0 224.3 jit_solution(14540871000820149885)
XLA Ops:
  0.6 1.3 broadcast_in_dim.2.gain_ref
  1.9 1.6 copy.16.res_ref
  3.6 1.9 copy.17.wo_ref
  5.5 2.4 %copy.18.wd_ref = bf16[1200,448]{1,0:T(8,128)(2,1)} copy(bf16[1200,448]{0,1:T(8,128)(2,1)} %param.27) | data formatting | bytes 2150400 | tf_op args[13]
  7.9 213.2 %layer.1 = (bf16[128,384]{1,0:T(8,128)(2,1)}, bf16[128,448]{1,0:T(8,128)(2,1)}) custom-call(bf16[128,384]{1,0:T(8,128)(2,1)} %q_ref.1, bf16[256,1024]{1,0:T(8,128)(2,1)} %key_ref.1, bf16[256,1024]{1,0:T(8,128)(2,1)} %value_ref.1, s32[16,128]{1,0:T(8,128)} %bitcast.6, s32[16,128]{1,0:T(8,128)} %bitcast.7, s32[32,128]{1,0:T(8,128)} %bitcast.4, ...), custom_call_target="tpu_custom_call" | custom-call | flops 8999999488 | bytes 8000000 | tf_op jit(solution)/shard_map/layer/pallas_call | solution.py:630
  221.0 1.7 copy.19
  222.7 1.5 copy.21

commit v2 on v1

v2 whole, which is shorter than its diff:
```python
import math

import jax
import jax.numpy as jnp
from jax import lax
from jax.experimental import pallas as pl
from jax.experimental.pallas import tpu as pltpu
from jax.sharding import PartitionSpec as P

MESH = pl.DeviceIdType.MESH
F32 = jnp.float32
BF16 = jnp.bfloat16

D = 7168
DH = 128
TILE = 128
SINK = 4
ROWS = 128
HALF = ROWS // 2
QUARTER = HALF // 2
NH = 3
KROWS = 256
COLS = 448
CC = 2 * COLS
FF = 1200
BLOCKS = 8

BLOCKED = -1e30
SCORE_SCALE = math.log2(math.e) / math.sqrt(DH)

N_COPIES = 260


def layer_kernel(
    q_ref,
    key_ref,
    value_ref,
    qspan_ref,
    qpos_ref,
    kspan_ref,
    kpos_ref,
    table_ref,
    res_ref,
    wo_ref,
    gain_ref,
    wg_ref,
    wu_ref,
    wd_ref,
    att_out,
    mix_out,
    kv,
    q3,
    m_s,
    l_s,
    acc_s,
    att,
    wo2,
    wd2,
    wg2,
    wu2,
    res2,
    gain2,
    res_s,
    part,
    half_in,
    full_in,
    z_out,
    z_in,
    total_s,
    stream,
    sq_out,
    sq_in,
    normed,
    gu,
    gu_half,
    gu_full,
    gu_z,
    hid,
    part2,
    half_in2,
    full_in2,
    z_out2,
    z_in2,
    total_s2,
    mixed_s,
    mix_t,
    mix_recv,
    send_sem,
    recv_sem,
    local_sem,
):
    c = lax.axis_index("context")
    t = lax.axis_index("tensor")
    y, z, k = c // 4, lax.rem(c // 2, 2), lax.rem(c, 2)
    zl, x = t // 4, lax.rem(t, 4)
    yp, ym, yo = lax.rem(y + 1, 4), lax.rem(y + 3, 4), lax.rem(y + 2, 4)
    xp, xm = lax.rem(x + 1, 4), lax.rem(x + 3, 4)
    zo, ko = 1 - z, 1 - k

    def dev(y_=None, z_=None, k_=None, zl_=None, x_=None):
        y_ = y if y_ is None else y_
        z_ = z if z_ is None else z_
        k_ = k if k_ is None else k_
        zl_ = zl if zl_ is None else zl_
        x_ = x if x_ is None else x_
        return (4 * y_ + 2 * z_ + k_, 4 * zl_ + x_)

    sibling, across = dev(k_=ko), dev(z_=zo)
    up_y, down_y = dev(y_=yp), dev(y_=ym)
    up_x, down_x = dev(x_=xp), dev(x_=xm)
    zl_peers = [dev(zl_=lax.rem(zl + d, 4)) for d in (1, 2, 3)]
    norm_peers = [
        dev(y_=lax.rem(y + dy, 4), z_=lax.rem(z + dz, 2))
        for dy in range(4)
        for dz in range(2)
        if dy or dz
    ]
    is_home = lax.rem(x + k, 2) == 0
    is_relay = lax.rem(x + k, 2) == 1

    count = [0]
    sent = []

    def numbers(*shape):
        base = count[0]
        count[0] += math.prod(shape)

        def at(*index):
            flat = 0
            for size, one in zip(shape, index):
                flat = flat * size + one
            return base + flat

        return at

    def copy(src, dst, to, number):
        return pltpu.make_async_remote_copy(
            src_ref=src,
            dst_ref=dst,
            send_sem=send_sem.at[number],
            recv_sem=recv_sem.at[number],
            device_id=to,
            device_id_type=MESH,
        )

    def send(src, dst, to, number):
        one = copy(src, dst, to, number)
        one.start()
        sent.append(one)

    def arrived(dst, number):
        copy(dst, dst, sibling, number).wait_recv()

    kv_head = t // 2
    head_columns = pl.ds(pl.multiple_of(kv_head * DH, DH), DH)
    my_rows = pl.ds(pl.multiple_of(k * COLS, COLS), COLS)
    loads = [
        pltpu.make_async_copy(key_ref.at[:, head_columns], kv.at[c, :, 0:DH], local_sem.at[0]),
        pltpu.make_async_copy(
            value_ref.at[:, head_columns], kv.at[c, :, DH : 2 * DH], local_sem.at[1]
        ),
        pltpu.make_async_copy(wo_ref, wo2.at[my_rows], local_sem.at[2]),
        pltpu.make_async_copy(res_ref, res2.at[my_rows], local_sem.at[3]),
        pltpu.make_async_copy(gain_ref, gain2.at[k], local_sem.at[4]),
        pltpu.make_async_copy(wg_ref, wg2.at[my_rows], local_sem.at[5]),
        pltpu.make_async_copy(wu_ref, wu2.at[my_rows], local_sem.at[6]),
        pltpu.make_async_copy(wd_ref, wd2.at[my_rows], local_sem.at[7]),
    ]
    for one in loads:
        one.start()

    barrier = pltpu.get_barrier_semaphore()
    peers = [sibling, up_x, down_x] + zl_peers + norm_peers
    for peer in peers:
        pl.semaphore_signal(barrier, inc=1, device_id=peer, device_id_type=MESH)
    pl.semaphore_wait(barrier, len(peers))

    loads[0].wait()
    loads[1].wait()
    kv_id = numbers(17)
    ids = [kv_id(n) for n in range(17)]

    def block_at(y_, z_, k_):
        return kv.at[4 * y_ + 2 * z_ + k_]

    def half_at(y_, z_, k_, h):
        return kv.at[4 * y_ + 2 * z_ + k_, h * (KROWS // 2) : (h + 1) * (KROWS // 2)]

    own = block_at(y, z, k)
    send(own, own, across, ids[0])
    send(own, own, up_y, ids[1])
    send(own, own, down_y, ids[2])
    send(own, own, sibling, ids[3])

    other = block_at(y, zo, k)
    arrived(other, ids[0])
    send(other, other, up_y, ids[4])
    send(other, other, down_y, ids[5])
    send(other, other, sibling, ids[6])
    b = block_at(ym, z, k)
    arrived(b, ids[1])
    send(half_at(ym, z, k, 0), half_at(ym, z, k, 0), up_y, ids[7])
    send(b, b, sibling, ids[9])
    b = block_at(yp, z, k)
    arrived(b, ids[2])
    send(half_at(yp, z, k, 1), half_at(yp, z, k, 1), down_y, ids[8])
    send(b, b, sibling, ids[10])
    b = block_at(ym, zo, k)
    arrived(b, ids[4])
    send(half_at(ym, zo, k, 0), half_at(ym, zo, k, 0), up_y, ids[11])
    send(b, b, sibling, ids[13])
    b = block_at(yp, zo, k)
    arrived(b, ids[5])
    send(half_at(yp, zo, k, 1), half_at(yp, zo, k, 1), down_y, ids[12])
    send(b, b, sibling, ids[14])

    for one in loads[2:]:
        one.wait()
    weight_id = numbers(6)
    half_rows = pl.ds(pl.multiple_of(k * COLS, COLS), COLS)
    other_rows = pl.ds(pl.multiple_of(ko * COLS, COLS), COLS)
    joint = (wo2, res2, wg2, wu2, wd2)
    for n, weights in enumerate(joint):
        send(weights.at[half_rows], weights.at[half_rows], sibling, weight_id(n))
    send(gain2.at[k], gain2.at[k], sibling, weight_id(5))

    for h in range(NH):
        q3[h] = q_ref[:, h * DH : (h + 1) * DH]
    m_s[...] = jnp.full(m_s.shape, BLOCKED, F32)
    l_s[...] = jnp.zeros(l_s.shape, F32)
    acc_s[...] = jnp.zeros(acc_s.shape, F32)

    def as_column(row):
        return jnp.broadcast_to(row.astype(F32), (ROWS, ROWS)).T.astype(jnp.int32)

    q_span = as_column(qspan_ref[pl.ds(c, 1), :])
    q_pos = as_column(qpos_ref[pl.ds(c, 1), :])

    def attend(group):
        visible = []
        for n in range(8):
            tile = 8 * group + n
            allowed = table_ref[c, tile] == 1
            spans = jnp.where(allowed, kspan_ref[pl.ds(tile, 1), :], -1)
            places = kpos_ref[pl.ds(tile, 1), :]
            index = tile * TILE + lax.broadcasted_iota(jnp.int32, (1, TILE), 1)
            spans = jnp.broadcast_to(spans, (ROWS, TILE))
            places = jnp.broadcast_to(places, (ROWS, TILE))
            index = jnp.broadcast_to(index, (ROWS, TILE))
            visible.append(
                jnp.where(
                    ((spans == q_span) & (places < q_pos)) | (index < SINK), 0.0, BLOCKED
                ).astype(F32)
            )
        keys = kv[pl.ds(4 * group, 4)].reshape(4 * KROWS, 2 * DH)

        def one_head(h, carry):
            scores = lax.dot_general(
                q3[h], keys[:, :DH], (((1,), (1,)), ((), ())), preferred_element_type=F32
            )
            pieces = [
                jnp.where(
                    visible[n] == 0.0,
                    scores[:, n * TILE : (n + 1) * TILE] * SCORE_SCALE,
                    BLOCKED,
                )
                for n in range(8)
            ]
            best = pieces[0]
            for piece in pieces[1:]:
                best = jnp.maximum(best, piece)
            old = m_s[h]
            new = jnp.maximum(old, jnp.max(best, axis=1, keepdims=True))
            factor = jnp.exp2(old - new)
            weights = [jnp.exp2(piece - new) for piece in pieces]
            total = weights[0]
            for one in weights[1:]:
                total = total + one
            m_s[h] = new
            l_s[h] = l_s[h] * factor + total
            rounded = jnp.concatenate([one.astype(BF16) for one in weights], axis=1)
            acc_s[h] = acc_s[h] * factor + jnp.dot(
                rounded, keys[:, DH:], preferred_element_type=F32
            )
            return carry

        lax.fori_loop(0, NH, one_head, 0)

    arrived(block_at(y, z, ko), ids[3])
    arrived(block_at(y, zo, ko), ids[6])
    attend(y)

    arrived(half_at(yo, z, k, 0), ids[7])
    arrived(half_at(yo, z, k, 1), ids[8])
    b = block_at(yo, z, k)
    send(b, b, sibling, ids[15])
    arrived(half_at(yo, zo, k, 0), ids[11])
    arrived(half_at(yo, zo, k, 1), ids[12])
    b = block_at(yo, zo, k)
    send(b, b, sibling, ids[16])

    arrived(block_at(ym, z, ko), ids[9])
    arrived(block_at(ym, zo, ko), ids[13])
    attend(ym)
    arrived(block_at(yp, z, ko), ids[10])
    arrived(block_at(yp, zo, ko), ids[14])
    attend(yp)
    arrived(block_at(yo, z, ko), ids[15])
    arrived(block_at(yo, zo, ko), ids[16])
    attend(yo)

    mine = 2 * y + z
    for h in range(NH):
        total = jnp.sum(l_s[h], axis=1, keepdims=True)
        att[mine, :, h * DH : (h + 1) * DH] = (acc_s[h] / total).astype(BF16)

    def gather_context(whole, piece, id_at, ready):
        own = whole(y, z)
        send(own, own, across, id_at(0))
        send(own, own, up_y, id_at(1))
        send(own, own, down_y, id_at(2))
        ready(y, z)
        yield
        b = whole(y, zo)
        arrived(b, id_at(0))
        send(b, b, up_y, id_at(3))
        send(b, b, down_y, id_at(4))
        for zz, first, then in ((z, 1, 5), (zo, 3, 7)):
            arrived(whole(ym, zz), id_at(first))
            send(piece(ym, zz, 0), piece(ym, zz, 0), up_y, id_at(then))
            arrived(whole(yp, zz), id_at(first + 1))
            send(piece(yp, zz, 1), piece(yp, zz, 1), down_y, id_at(then + 1))
            if first == 1:
                ready(y, zo)
            ready(ym, zz)
            ready(yp, zz)
        for zz, then in ((z, 5), (zo, 7)):
            arrived(piece(yo, zz, 0), id_at(then))
            arrived(piece(yo, zz, 1), id_at(then + 1))
            ready(yo, zz)

    def lagged(lag, work):
        waiting = []

        def add(*one):
            waiting.append(one)
            if len(waiting) > lag:
                work(*waiting.pop(0))

        def flush():
            while waiting:
                work(*waiting.pop(0))

        return add, flush

    home_j = x // 2
    plus_j, minus_j = xp // 2, xm // 2
    order = [(d, lax.rem(zl + d, 4)) for d in (2, 1, 3, 0)]

    class Scatter:
        def __init__(self, shares, halves, fulls, out, inn, total):
            self.shares, self.halves, self.fulls = shares, halves, fulls
            self.out, self.inn, self.total = out, inn, total
            self.half_id = numbers(2, 4, 2)
            self.full_id = numbers(2, 4, 2)
            self.z_id = numbers(2, 3)

        def half(self, h, to, way):
            rows = slice(way * QUARTER, (way + 1) * QUARTER)
            return copy(
                self.shares.at[h, 2 * to + 1 - home_j, rows],
                self.halves.at[h, way, to],
                (up_x, down_x)[way],
                self.half_id(h, to, way),
            )

        def full(self, h, to, way):
            return copy(
                self.shares.at[h, 2 * to + (plus_j, minus_j)[way]],
                self.fulls.at[h, way, to],
                (up_x, down_x)[way],
                self.full_id(h, to, way),
            )

        def along_z(self, h, d):
            return copy(
                self.out.at[h, d - 1], self.inn.at[h, d - 1], zl_peers[d - 1], self.z_id(h, d - 1)
            )

        def ready(self, h, to, j):
            @pl.when(is_home & (j == 1 - home_j))
            def _():
                self.half(h, to, 0).start()
                self.half(h, to, 1).start()

        def relay(self, h, to, j):
            for way, at in ((0, plus_j), (1, minus_j)):
                rows = slice(way * QUARTER, (way + 1) * QUARTER)

                @pl.when(is_relay & (j == at))
                def _():
                    i = 2 * to + at
                    arrived(self.halves.at[h, way, to], self.half_id(h, to, way))
                    self.shares[h, i, rows] = (
                        self.shares[h, i, rows].astype(F32) + self.halves[h, way, to].astype(F32)
                    ).astype(BF16)
                    self.full(h, to, way).start()

        def finish_x(self, h):
            for d, to in order:
                arrived(self.fulls.at[h, 0, to], self.full_id(h, to, 0))
                arrived(self.fulls.at[h, 1, to], self.full_id(h, to, 1))
                here = (
                    self.shares[h, 2 * to + home_j].astype(F32)
                    + self.fulls[h, 0, to].astype(F32)
                    + self.fulls[h, 1, to].astype(F32)
                )
                if d:
                    self.out[h, d - 1] = here.astype(BF16)
                    self.along_z(h, d).start()
                else:
                    self.total[h] = here

        def finish_z(self, h):
            total = self.total[h]
            for d in (1, 3, 2):
                arrived(self.inn.at[h, d - 1], self.z_id(h, d - 1))
                total = total + self.inn[h, d - 1].astype(F32)
            return total

        def wait_sends(self):
            @pl.when(is_home)
            def _():
                for h in range(2):
                    for d in range(4):
                        self.half(h, d, 0).wait_send()
                        self.half(h, d, 1).wait_send()
                    for d in (1, 2, 3):
                        self.along_z(h, d).wait_send()

            @pl.when(is_relay)
            def _():
                for h in range(2):
                    for d in range(4):
                        self.full(h, d, 0).wait_send()
                        self.full(h, d, 1).wait_send()

    projected = Scatter(part, half_in, full_in, z_out, z_in, total_s)
    arrived(wo2.at[other_rows], weight_id(0))
    seen = []
    relay_a, flush_a = lagged(2, lambda to, j: projected.relay(0, to, j))

    def project(to, j):
        i = 2 * to + j
        rows = lax.dot_general(
            att[i], wo2[...], (((1,), (1,)), ((), ())), preferred_element_type=F32
        ).astype(BF16)
        part[0, i] = rows[:HALF]
        part[1, i] = rows[HALF:]
        projected.ready(0, to, j)
        seen.append((to, j))
        relay_a(to, j)

    for _ in gather_context(
        lambda y_, z_: att.at[2 * y_ + z_],
        lambda y_, z_, h: att.at[2 * y_ + z_, h * HALF : (h + 1) * HALF],
        numbers(9),
        project,
    ):
        pass
    for to, j in seen:
        projected.ready(1, to, j)
    flush_a()
    for to, j in seen:
        projected.relay(1, to, j)
    att_out[...] = att[mine]

    norm_id = numbers(2, 7)
    gather_z_id = numbers(2, 3)
    gather_x_id = numbers(2, 4, 2)
    gather_half_id = numbers(2, 4, 2)
    arrived(res2.at[other_rows], weight_id(1))
    arrived(gain2.at[ko], weight_id(5))

    def square(h, n):
        return copy(sq_out.at[h], sq_in.at[h, n], norm_peers[n], norm_id(h, n))

    def gather_z(h, d):
        own = normed.at[h, 2 * zl + home_j]
        return copy(own, own, zl_peers[d - 1], gather_z_id(h, d - 1))

    def gather_x(h, zq, way):
        b = normed.at[h, 2 * zq + home_j]
        return copy(b, b, (up_x, down_x)[way], gather_x_id(h, zq, way))

    def gather_half(h, zq, way):
        j = (minus_j, plus_j)[way]
        b = normed.at[h, 2 * zq + j, way * QUARTER : (way + 1) * QUARTER]
        return copy(b, b, (up_x, down_x)[way], gather_half_id(h, zq, way))

    def sum_squares(h):
        total = projected.finish_z(h)
        rounded = (res_s[h] + total).astype(BF16)
        stream[h] = rounded
        st = rounded.astype(F32)
        squares = jnp.sum(st * st, axis=1, keepdims=True)
        squares = jnp.concatenate([squares, squares], axis=0)
        sq_out[h] = jnp.broadcast_to(squares, (ROWS, ROWS)).T[0:8]
        for n in range(7):
            square(h, n).start()

    def normalise(h):
        whole = sq_out[h]
        for n in range(7):
            arrived(sq_in.at[h, n], norm_id(h, n))
            whole = whole + sq_in[h, n]
        column = jnp.broadcast_to(whole[0:1], (ROWS, ROWS)).T[0:HALF, 0:1]
        gain = jnp.concatenate([gain2[0][0:1], gain2[1][0:1]], axis=1)
        st = stream[h].astype(F32)
        normed[h, 2 * zl + home_j] = (st * lax.rsqrt(column / D + 1e-05) * gain).astype(BF16)
        for way in range(2):
            gather_x(h, zl, way).start()
        for d in (2, 1, 3):
            gather_z(h, d).start()

    @pl.when(is_home)
    def _():
        rows = res2[...].astype(F32).T
        res_s[0] = rows[:HALF]
        res_s[1] = rows[HALF:]
        projected.finish_x(0)
        sum_squares(0)
        projected.finish_x(1)
        normalise(0)

    arrived(wg2.at[other_rows], weight_id(2))
    arrived(wu2.at[other_rows], weight_id(3))
    half_id = numbers(2, 2, 2)
    full_id = numbers(2, 2, 2)
    cross_id = numbers(2)
    first_j = jnp.where(is_home, home_j, minus_j)

    def y_half(h, zz, way):
        rows = slice(way * QUARTER, (way + 1) * QUARTER)
        return copy(
            gu.at[h, 2 * yo + zz, :, rows],
            gu_half.at[h, way, zz],
            (up_y, down_y)[way],
            half_id(h, zz, way),
        )

    def y_full(h, zz, way):
        return copy(
            gu.at[h, 2 * (yp, ym)[way] + zz],
            gu_full.at[h, way, zz],
            (up_y, down_y)[way],
            full_id(h, zz, way),
        )

    def y_cross(h):
        return copy(gu.at[h, 2 * y + zo], gu_z.at[h], across, cross_id(h))

    def gate_up(h, zq, j):
        i = 2 * zq + j
        rows = normed[h, i]
        gu[h, i, 0] = jnp.dot(rows, wg2[...], preferred_element_type=F32).astype(BF16)
        gu[h, i, 1] = jnp.dot(rows, wu2[...], preferred_element_type=F32).astype(BF16)

        @pl.when(lax.rem(zq - y + 4, 4) == 2)
        def _():
            y_half(h, j, 0).start()
            y_half(h, j, 1).start()

    def steps_back(n):
        d = jnp.where(n < 2, n, 5 - n)
        return d, lax.rem(zl + 4 - d, 4)

    def take_first(h, n):
        d, zq = steps_back(n)

        @pl.when(is_home & (n > 0))
        def _():
            arrived(normed.at[h, 2 * zq + home_j], gather_z_id(h, d - 1))
            gather_x(h, zq, 0).start()
            gather_x(h, zq, 1).start()

        @pl.when(is_relay)
        def _():
            arrived(normed.at[h, 2 * zq + minus_j], gather_x_id(h, zq, 0))
            gather_half(h, zq, 0).start()
            arrived(normed.at[h, 2 * zq + plus_j], gather_x_id(h, zq, 1))
            gather_half(h, zq, 1).start()

        gate_up(h, zq, first_j)

    def take_second(h, n):
        d, zq = steps_back(n)

        @pl.when(is_home)
        def _():
            for way in range(2):
                b = normed.at[h, 2 * zq + 1 - home_j, way * QUARTER : (way + 1) * QUARTER]
                arrived(b, gather_half_id(h, zq, way))

        gate_up(h, zq, 1 - first_j)

    def y_relay(h, n):
        d, zq = steps_back(n)
        for way, there in ((0, yp), (1, ym)):
            rows = slice(way * QUARTER, (way + 1) * QUARTER)

            @pl.when(zq == there)
            def _():
                for zz in range(2):
                    i = 2 * there + zz
                    arrived(gu_half.at[h, way, zz], half_id(h, zz, way))
                    gu[h, i, :, rows] = (
                        gu[h, i, :, rows].astype(F32) + gu_half[h, way, zz].astype(F32)
                    ).astype(BF16)
                    y_full(h, zz, way).start()

    def own_sum(h, zz, which):
        return (
            gu[h, 2 * y + zz, which].astype(F32)
            + gu_full[h, 0, zz, which].astype(F32)
            + gu_full[h, 1, zz, which].astype(F32)
        )

    def finish_y_across(h):
        arrived(gu_full.at[h, 0, zo], full_id(h, zo, 0))
        arrived(gu_full.at[h, 1, zo], full_id(h, zo, 1))
        for which in range(2):
            gu[h, 2 * y + zo, which] = own_sum(h, zo, which).astype(BF16)
        y_cross(h).start()

    def finish_y(h):
        arrived(gu_full.at[h, 0, z], full_id(h, z, 0))
        arrived(gu_full.at[h, 1, z], full_id(h, z, 1))
        arrived(gu_z.at[h], cross_id(h))
        gate = own_sum(h, z, 0) + gu_z[h, 0].astype(F32)
        up = own_sum(h, z, 1) + gu_z[h, 1].astype(F32)
        hid[h, mine] = (gate / (1.0 + jnp.exp(-gate)) * up).astype(BF16)

    def steps_a(n, carry):
        @pl.when(n < 4)
        def _():
            take_first(0, n)

        @pl.when(is_home & (n == 1))
        def _():
            sum_squares(1)

        @pl.when(is_home & (n == 2))
        def _():
            normalise(1)

        @pl.when((n >= 1) & (n < 5))
        def _():
            take_second(0, n - 1)

        @pl.when(n >= 2)
        def _():
            y_relay(0, n - 2)

        return carry

    def steps_b(n, carry):
        @pl.when(n < 4)
        def _():
            take_first(1, n)

        @pl.when(n >= 1)
        def _():
            take_second(1, n - 1)

        return carry

    lax.fori_loop(0, 6, steps_a, 0)
    lax.fori_loop(0, 5, steps_b, 0)
    finish_y_across(0)
    for n in range(4):
        y_relay(1, n)

    arrived(wd2.at[other_rows], weight_id(4))
    summed = Scatter(part2, half_in2, full_in2, z_out2, z_in2, total_s2)

    def spread_hidden(h):
        relay, flush = lagged(2, lambda to, j: summed.relay(h, to, j))

        def down(to, j):
            i = 2 * to + j
            part2[h, i] = lax.dot_general(
                hid[h, i], wd2[...], (((1,), (1,)), ((), ())), preferred_element_type=F32
            ).astype(BF16)
            summed.ready(h, to, j)
            relay(to, j)

        yield from gather_context(
            lambda y_, z_: hid.at[h, 2 * y_ + z_],
            lambda y_, z_, q: hid.at[h, 2 * y_ + z_, q * QUARTER : (q + 1) * QUARTER],
            numbers(9),
            down,
        )
        flush()

    finish_y(0)
    spread_a, spread_b = spread_hidden(0), spread_hidden(1)
    next(spread_a)
    finish_y_across(1)
    for _ in spread_a:
        pass
    finish_y(1)
    next(spread_b)

    @pl.when(is_home)
    def _():
        summed.finish_x(0)

    for _ in spread_b:
        pass

    mix_id = numbers(1)(0)
    mix_mine = mix_t.at[other_rows]

    @pl.when(is_home)
    def _():
        mixed_s[0] = stream[0].astype(F32) + summed.finish_z(0)
        summed.finish_x(1)
        mixed_s[1] = stream[1].astype(F32) + summed.finish_z(1)
        mixed = jnp.concatenate([mixed_s[0], mixed_s[1]], axis=0)
        mix_t[...] = mixed.T.astype(BF16)
        copy(mix_mine, mix_recv, sibling, mix_id).start()
        mix_out[...] = mix_t[half_rows]
        copy(mix_mine, mix_recv, sibling, mix_id).wait_send()

    @pl.when(is_relay)
    def _():
        arrived(mix_recv, mix_id)
        mix_out[...] = mix_recv[...]

    for one in sent:
        one.wait_send()
    projected.wait_sends()
    summed.wait_sends()
    for h in range(2):
        for zz in range(2):
            for way in range(2):
                y_half(h, zz, way).wait_send()
                y_full(h, zz, way).wait_send()
        y_cross(h).wait_send()

    @pl.when(is_home)
    def _():
        for h in range(2):
            for n in range(7):
                square(h, n).wait_send()
            for d in (1, 2, 3):
                gather_z(h, d).wait_send()
            for zq in range(4):
                for way in range(2):
                    gather_x(h, zq, way).wait_send()

    @pl.when(is_relay)
    def _():
        for h in range(2):
            for zq in range(4):
                for way in range(2):
                    gather_half(h, zq, way).wait_send()

    assert count[0] <= N_COPIES


def local(
    queries,
    context_keys,
    context_values,
    query_span,
    query_position,
    key_span,
    key_position,
    tile_table,
    residual,
    out_weight,
    norm_gain,
    gate_weight,
    up_weight,
    down_weight,
):
    vmem = pl.BlockSpec(memory_space=pltpu.VMEM)
    smem = pl.BlockSpec(memory_space=pltpu.SMEM)
    hbm = pl.BlockSpec(memory_space=pl.ANY)
    gain = jnp.broadcast_to(norm_gain.astype(F32)[None, :], (8, COLS))
    def stages():
        return [
            pltpu.VMEM((2, BLOCKS, HALF, CC), BF16),
            pltpu.VMEM((2, 2, 4, QUARTER, CC), BF16),
            pltpu.VMEM((2, 2, 4, HALF, CC), BF16),
            pltpu.VMEM((2, 3, HALF, CC), BF16),
            pltpu.VMEM((2, 3, HALF, CC), BF16),
            pltpu.VMEM((2, HALF, CC), F32),
        ]

    scratch = [
        pltpu.VMEM((16, KROWS, 2 * DH), BF16),
        pltpu.VMEM((NH, ROWS, DH), BF16),
        pltpu.VMEM((NH, ROWS, DH), F32),
        pltpu.VMEM((NH, ROWS, DH), F32),
        pltpu.VMEM((NH, ROWS, DH), F32),
        pltpu.VMEM((BLOCKS, ROWS, NH * DH), BF16),
        pltpu.VMEM((CC, NH * DH), BF16),
        pltpu.VMEM((CC, FF), BF16),
        pltpu.VMEM((CC, FF), BF16),
        pltpu.VMEM((CC, FF), BF16),
        pltpu.VMEM((CC, ROWS), BF16),
        pltpu.VMEM((2, 8, COLS), F32),
        pltpu.VMEM((2, HALF, CC), F32),
        *stages(),
        pltpu.VMEM((2, HALF, CC), BF16),
        pltpu.VMEM((2, 8, ROWS), F32),
        pltpu.VMEM((2, 7, 8, ROWS), F32),
        pltpu.VMEM((2, BLOCKS, HALF, CC), BF16),
        pltpu.VMEM((2, BLOCKS, 2, HALF, FF), BF16),
        pltpu.VMEM((2, 2, 2, 2, QUARTER, FF), BF16),
        pltpu.VMEM((2, 2, 2, 2, HALF, FF), BF16),
        pltpu.VMEM((2, 2, HALF, FF), BF16),
        pltpu.VMEM((2, BLOCKS, HALF, FF), BF16),
        *stages(),
        pltpu.VMEM((2, HALF, CC), F32),
        pltpu.VMEM((CC, ROWS), BF16),
        pltpu.VMEM((COLS, ROWS), BF16),
        pltpu.SemaphoreType.DMA((N_COPIES,)),
        pltpu.SemaphoreType.DMA((N_COPIES,)),
        pltpu.SemaphoreType.DMA((8,)),
    ]
    attention, mixed = pl.pallas_call(
        layer_kernel,
        out_shape=(
            jax.ShapeDtypeStruct(queries.shape, BF16),
            jax.ShapeDtypeStruct(residual.shape[::-1], BF16),
        ),
        in_specs=[vmem, hbm, hbm, vmem, vmem, vmem, vmem, smem, hbm, hbm, hbm, hbm, hbm, hbm],
        out_specs=(vmem, vmem),
        scratch_shapes=scratch,
        compiler_params=pltpu.CompilerParams(
            collective_id=0, has_side_effects=True, vmem_limit_bytes=60 * 2**20
        ),
        cost_estimate=pl.CostEstimate(
            flops=9_000_000_000, bytes_accessed=8_000_000, transcendentals=2_000_000
        ),
        name="layer",
    )(
        queries,
        context_keys,
        context_values,
        query_span.reshape(16, TILE),
        query_position.reshape(16, TILE),
        key_span.reshape(32, TILE),
        key_position.reshape(32, TILE),
        tile_table,
        residual.T,
        out_weight.T,
        gain,
        gate_weight,
        up_weight,
        down_weight.T,
    )
    return attention, mixed.T


def solution(mesh):
    placed = (
        P("context", "tensor"),
        P("context", None),
        P("context", None),
        P(),
        P(),
        P(),
        P(),
        P(),
        P("tensor", "context"),
        P("tensor", "context"),
        P("context"),
        P("context", "tensor"),
        P("context", "tensor"),
        P("tensor", "context"),
    )
    return jax.shard_map(
        local,
        mesh=mesh,
        in_specs=placed,
        out_specs=(P("context", "tensor"), P("tensor", "context")),
        check_vma=False,
    )
```

time: 228 us -> 205 us (0.90)
  Pallas kernels: 213 us -> 198 us
  local copies, waits for them, and re-layouts: 10.4 us -> 4.38 us
    pallas_call x1, Pallas kernels: 213 us -> 198 us  [local(): pl.pallas_call(layer_kernel, out_shape=(jax.ShapeDtypeStruct(queries.shap...]
    unnamed x4 -> x2, local copies, waits for them, and re-layouts: 7.49 us -> 3.09 us
where the time goes in v2:
time: 205 us; the launch traced here: 203 us
  Pallas kernels  198 us (97%)
  local copies, waits for them, and re-layouts  4.38 us (2%)
    pallas_call x1, Pallas kernels, local(): pl.pallas_call(layer_kernel, out_shape=(jax.ShapeDtypeStruct(queries.shap...  198 us

profile of v2, /device:TPU:16, one launch (start us, length us, event | category | flops | bytes accessed | tf_op | source)
XLA Modules:
  0.0 203.2 jit_solution(12069712075221500469)
XLA Ops:
  0.6 1.3 broadcast_in_dim.2.gain_ref
  1.9 198.2 %layer.1 = (bf16[128,384]{1,0:T(8,128)(2,1)}, bf16[448,128]{1,0:T(8,128)(2,1)}) custom-call(bf16[128,384]{1,0:T(8,128)(2,1)} %q_ref.1, bf16[256,1024]{1,0:T(8,128)(2,1)} %key_ref.1, bf16[256,1024]{1,0:T(8,128)(2,1)} %value_ref.1, s32[16,128]{1,0:T(8,128)} %bitcast.14, s32[16,128]{1,0:T(8,128)} %bitcast.15, s32[32,128]{1,0:T(8,128)} %bitcast.12, ...), custom_call_target="tpu_custom_call" | custom-call | flops 8999999488 | bytes 8000000 | tf_op jit(solution)/shard_map/layer/pallas_call | solution.py:835
  200.1 1.5 copy.18
  201.6 1.6 copy.19

commit v3 on v2

--- a/solution.py
+++ b/solution.py
@@ -23,6 +23,7 @@
 COLS = 448
 CC = 2 * COLS
 FF = 1200
+WIDE = 1280
 BLOCKS = 8
 
 BLOCKED = -1e30
@@ -59,7 +60,6 @@
     wg2,
     wu2,
     res2,
-    gain2,
     res_s,
     part,
     half_in,
@@ -67,9 +67,6 @@
     z_out,
     z_in,
     total_s,
-    stream,
-    sq_out,
-    sq_in,
     normed,
     gu,
     gu_half,
@@ -82,6 +79,7 @@
     z_out2,
     z_in2,
     total_s2,
+    wd_t,
     mixed_s,
     mix_t,
     mix_recv,
@@ -109,12 +107,6 @@
     up_y, down_y = dev(y_=yp), dev(y_=ym)
     up_x, down_x = dev(x_=xp), dev(x_=xm)
     zl_peers = [dev(zl_=lax.rem(zl + d, 4)) for d in (1, 2, 3)]
-    norm_peers = [
-        dev(y_=lax.rem(y + dy, 4), z_=lax.rem(z + dz, 2))
-        for dy in range(4)
-        for dz in range(2)
-        if dy or dz
-    ]
     is_home = lax.rem(x + k, 2) == 0
     is_relay = lax.rem(x + k, 2) == 1
 
@@ -161,16 +153,15 @@
         ),
         pltpu.make_async_copy(wo_ref, wo2.at[my_rows], local_sem.at[2]),
         pltpu.make_async_copy(res_ref, res2.at[my_rows], local_sem.at[3]),
-        pltpu.make_async_copy(gain_ref, gain2.at[k], local_sem.at[4]),
-        pltpu.make_async_copy(wg_ref, wg2.at[my_rows], local_sem.at[5]),
-        pltpu.make_async_copy(wu_ref, wu2.at[my_rows], local_sem.at[6]),
-        pltpu.make_async_copy(wd_ref, wd2.at[my_rows], local_sem.at[7]),
+        pltpu.make_async_copy(wg_ref, wg2.at[my_rows], local_sem.at[4]),
+        pltpu.make_async_copy(wu_ref, wu2.at[my_rows], local_sem.at[5]),
+        pltpu.make_async_copy(wd_ref, wd2.at[my_rows], local_sem.at[6]),
     ]
     for one in loads:
         one.start()
 
     barrier = pltpu.get_barrier_semaphore()
-    peers = [sibling, up_x, down_x] + zl_peers + norm_peers
+    peers = [sibling, across, up_y, down_y, up_x, down_x] + zl_peers
     for peer in peers:
         pl.semaphore_signal(barrier, inc=1, device_id=peer, device_id_type=MESH)
     pl.semaphore_wait(barrier, len(peers))
@@ -191,6 +182,12 @@
     send(own, own, up_y, ids[1])
     send(own, own, down_y, ids[2])
     send(own, own, sibling, ids[3])
+
+    for one in loads[2:]:
+        one.wait()
+    gain = jnp.broadcast_to(gain_ref[0:1, :], (DH, COLS)).T[:, 0:1]
+    for weights in (wg2, wu2):
+        weights[my_rows] = (weights[my_rows].astype(F32) * gain).astype(BF16)
 
     other = block_at(y, zo, k)
     arrived(other, ids[0])
@@ -214,15 +211,12 @@
     send(half_at(yp, zo, k, 1), half_at(yp, zo, k, 1), down_y, ids[12])
     send(b, b, sibling, ids[14])
 
-    for one in loads[2:]:
-        one.wait()
-    weight_id = numbers(6)
+    weight_id = numbers(5)
     half_rows = pl.ds(pl.multiple_of(k * COLS, COLS), COLS)
     other_rows = pl.ds(pl.multiple_of(ko * COLS, COLS), COLS)
     joint = (wo2, res2, wg2, wu2, wd2)
     for n, weights in enumerate(joint):
         send(weights.at[half_rows], weights.at[half_rows], sibling, weight_id(n))
-    send(gain2.at[k], gain2.at[k], sibling, weight_id(5))
 
     for h in range(NH):
         q3[h] = q_ref[:, h * DH : (h + 1) * DH]
@@ -355,15 +349,13 @@
 
     home_j = x // 2
     plus_j, minus_j = xp // 2, xm // 2
-    order = [(d, lax.rem(zl + d, 4)) for d in (2, 1, 3, 0)]
-
     class Scatter:
         def __init__(self, shares, halves, fulls, out, inn, total):
             self.shares, self.halves, self.fulls = shares, halves, fulls
             self.out, self.inn, self.total = out, inn, total
             self.half_id = numbers(2, 4, 2)
             self.full_id = numbers(2, 4, 2)
-            self.z_id = numbers(2, 3)
+            self.z_id = numbers(2, 4)
 
         def half(self, h, to, way):
             rows = slice(way * QUARTER, (way + 1) * QUARTER)
@@ -383,9 +375,8 @@
             )
 
         def along_z(self, h, d):
-            return copy(
-                self.out.at[h, d - 1], self.inn.at[h, d - 1], zl_peers[d - 1], self.z_id(h, d - 1)
-            )
+            to = dev(zl_=lax.rem(zl + d, 4))
+            return copy(self.out.at[h, d], self.inn.at[h, d], to, self.z_id(h, d))
 
         def ready(self, h, to, j):
             @pl.when(is_home & (j == 1 - home_j))
@@ -407,7 +398,7 @@
                     self.full(h, to, way).start()
 
         def finish_x(self, h):
-            for d, to in order:
+            for to in (y, ym, yp, yo):
                 arrived(self.fulls.at[h, 0, to], self.full_id(h, to, 0))
                 arrived(self.fulls.at[h, 1, to], self.full_id(h, to, 1))
                 here = (
@@ -415,17 +406,22 @@
                     + self.fulls[h, 0, to].astype(F32)
                     + self.fulls[h, 1, to].astype(F32)
                 )
-                if d:
-                    self.out[h, d - 1] = here.astype(BF16)
+
+                @pl.when(to == zl)
+                def _():
+                    self.total[h] = here
+
+                @pl.when(to != zl)
+                def _():
+                    d = lax.rem(to - zl + 4, 4)
+                    self.out[h, d] = here.astype(BF16)
                     self.along_z(h, d).start()
-                else:
-                    self.total[h] = here
 
         def finish_z(self, h):
             total = self.total[h]
             for d in (1, 3, 2):
-                arrived(self.inn.at[h, d - 1], self.z_id(h, d - 1))
-                total = total + self.inn[h, d - 1].astype(F32)
+                arrived(self.inn.at[h, d], self.z_id(h, d))
+                total = total + self.inn[h, d].astype(F32)
             return total
 
         def wait_sends(self):
@@ -475,15 +471,10 @@
         projected.relay(1, to, j)
     att_out[...] = att[mine]
 
-    norm_id = numbers(2, 7)
     gather_z_id = numbers(2, 3)
     gather_x_id = numbers(2, 4, 2)
     gather_half_id = numbers(2, 4, 2)
     arrived(res2.at[other_rows], weight_id(1))
-    arrived(gain2.at[ko], weight_id(5))
-
-    def square(h, n):
-        return copy(sq_out.at[h], sq_in.at[h, n], norm_peers[n], norm_id(h, n))
 
     def gather_z(h, d):
         own = normed.at[h, 2 * zl + home_j]
@@ -498,26 +489,9 @@
         b = normed.at[h, 2 * zq + j, way * QUARTER : (way + 1) * QUARTER]
         return copy(b, b, (up_x, down_x)[way], gather_half_id(h, zq, way))
 
-    def sum_squares(h):
+    def make_stream(h):
         total = projected.finish_z(h)
-        rounded = (res_s[h] + total).astype(BF16)
-        stream[h] = rounded
-        st = rounded.astype(F32)
-        squares = jnp.sum(st * st, axis=1, keepdims=True)
-        squares = jnp.concatenate([squares, squares], axis=0)
-        sq_out[h] = jnp.broadcast_to(squares, (ROWS, ROWS)).T[0:8]
-        for n in range(7):
-            square(h, n).start()
-
-    def normalise(h):
-        whole = sq_out[h]
-        for n in range(7):
-            arrived(sq_in.at[h, n], norm_id(h, n))
-            whole = whole + sq_in[h, n]
-        column = jnp.broadcast_to(whole[0:1], (ROWS, ROWS)).T[0:HALF, 0:1]
-        gain = jnp.concatenate([gain2[0][0:1], gain2[1][0:1]], axis=1)
-        st = stream[h].astype(F32)
-        normed[h, 2 * zl + home_j] = (st * lax.rsqrt(column / D + 1e-05) * gain).astype(BF16)
+        normed[h, 2 * zl + home_j] = (res_s[h] + total).astype(BF16)
         for way in range(2):
             gather_x(h, zl, way).start()
         for d in (2, 1, 3):
@@ -529,9 +503,8 @@
         res_s[0] = rows[:HALF]
         res_s[1] = rows[HALF:]
         projected.finish_x(0)
-        sum_squares(0)
+        make_stream(0)
         projected.finish_x(1)
-        normalise(0)
 
     arrived(wg2.at[other_rows], weight_id(2))
     arrived(wu2.at[other_rows], weight_id(3))
@@ -563,8 +536,11 @@
     def gate_up(h, zq, j):
         i = 2 * zq + j
         rows = normed[h, i]
-        gu[h, i, 0] = jnp.dot(rows, wg2[...], preferred_element_type=F32).astype(BF16)
-        gu[h, i, 1] = jnp.dot(rows, wu2[...], preferred_element_type=F32).astype(BF16)
+        wide = rows.astype(F32)
+        squares = jnp.broadcast_to(jnp.sum(wide * wide, axis=1, keepdims=True), (HALF, WIDE - FF))
+        gate = jnp.dot(rows, wg2[...], preferred_element_type=F32)
+        gu[h, i, 0] = jnp.concatenate([gate, squares], axis=1).astype(BF16)
+        gu[h, i, 1, :, :FF] = jnp.dot(rows, wu2[...], preferred_element_type=F32).astype(BF16)
 
         @pl.when(lax.rem(zq - y + 4, 4) == 2)
         def _():
@@ -611,7 +587,7 @@
 
             @pl.when(zq == there)
             def _():
-                for zz in range(2):
+                for zz in (zo, z):
                     i = 2 * there + zz
                     arrived(gu_half.at[h, way, zz], half_id(h, zz, way))
                     gu[h, i, :, rows] = (
@@ -638,7 +614,9 @@
         arrived(gu_full.at[h, 1, z], full_id(h, z, 1))
         arrived(gu_z.at[h], cross_id(h))
         gate = own_sum(h, z, 0) + gu_z[h, 0].astype(F32)
-        up = own_sum(h, z, 1) + gu_z[h, 1].astype(F32)
+        up = (own_sum(h, z, 1) + gu_z[h, 1].astype(F32))[:, :FF]
+        scale = lax.rsqrt(gate[:, FF : FF + 1] / D + 1e-05)
+        gate, up = gate[:, :FF] * scale, up * scale
         hid[h, mine] = (gate / (1.0 + jnp.exp(-gate)) * up).astype(BF16)
 
     def steps_a(n, carry):
@@ -648,19 +626,15 @@
 
         @pl.when(is_home & (n == 1))
         def _():
-            sum_squares(1)
-
-        @pl.when(is_home & (n == 2))
-        def _():
-            normalise(1)
-
-        @pl.when((n >= 1) & (n < 5))
+            make_stream(1)
+
+        @pl.when(n >= 1)
         def _():
             take_second(0, n - 1)
 
-        @pl.when(n >= 2)
-        def _():
-            y_relay(0, n - 2)
+        @pl.when(n >= 3)
+        def _():
+            y_relay(0, n - 3)
 
         return carry
 
@@ -669,19 +643,24 @@
         def _():
             take_first(1, n)
 
+        @pl.when(n < 2)
+        def _():
+            y_relay(0, n + 2)
+
         @pl.when(n >= 1)
         def _():
             take_second(1, n - 1)
 
         return carry
 
-    lax.fori_loop(0, 6, steps_a, 0)
+    lax.fori_loop(0, 5, steps_a, 0)
     lax.fori_loop(0, 5, steps_b, 0)
+    arrived(wd2.at[other_rows], weight_id(4))
+    wd_t[...] = wd2[...].T
     finish_y_across(0)
     for n in range(4):
         y_relay(1, n)
 
-    arrived(wd2.at[other_rows], weight_id(4))
     summed = Scatter(part2, half_in2, full_in2, z_out2, z_in2, total_s2)
 
     def spread_hidden(h):
@@ -689,9 +668,7 @@
 
         def down(to, j):
             i = 2 * to + j
-            part2[h, i] = lax.dot_general(
-                hid[h, i], wd2[...], (((1,), (1,)), ((), ())), preferred_element_type=F32
-            ).astype(BF16)
+            part2[h, i] = jnp.dot(hid[h, i], wd_t[...], preferred_element_type=F32).astype(BF16)
             summed.ready(h, to, j)
             relay(to, j)
 
@@ -724,9 +701,9 @@
 
     @pl.when(is_home)
     def _():
-        mixed_s[0] = stream[0].astype(F32) + summed.finish_z(0)
+        mixed_s[0] = normed[0, 2 * zl + home_j].astype(F32) + summed.finish_z(0)
         summed.finish_x(1)
-        mixed_s[1] = stream[1].astype(F32) + summed.finish_z(1)
+        mixed_s[1] = normed[1, 2 * zl + home_j].astype(F32) + summed.finish_z(1)
         mixed = jnp.concatenate([mixed_s[0], mixed_s[1]], axis=0)
         mix_t[...] = mixed.T.astype(BF16)
         copy(mix_mine, mix_recv, sibling, mix_id).start()
@@ -752,8 +729,6 @@
     @pl.when(is_home)
     def _():
         for h in range(2):
-            for n in range(7):
-                square(h, n).wait_send()
             for d in (1, 2, 3):
                 gather_z(h, d).wait_send()
             for zq in range(4):
@@ -795,8 +770,8 @@
             pltpu.VMEM((2, BLOCKS, HALF, CC), BF16),
             pltpu.VMEM((2, 2, 4, QUARTER, CC), BF16),
             pltpu.VMEM((2, 2, 4, HALF, CC), BF16),
-            pltpu.VMEM((2, 3, HALF, CC), BF16),
-            pltpu.VMEM((2, 3, HALF, CC), BF16),
+            pltpu.VMEM((2, 4, HALF, CC), BF16),
+            pltpu.VMEM((2, 4, HALF, CC), BF16),
             pltpu.VMEM((2, HALF, CC), F32),
         ]
 
@@ -812,19 +787,16 @@
         pltpu.VMEM((CC, FF), BF16),
         pltpu.VMEM((CC, FF), BF16),
         pltpu.VMEM((CC, ROWS), BF16),
-        pltpu.VMEM((2, 8, COLS), F32),
         pltpu.VMEM((2, HALF, CC), F32),
         *stages(),
-        pltpu.VMEM((2, HALF, CC), BF16),
-        pltpu.VMEM((2, 8, ROWS), F32),
-        pltpu.VMEM((2, 7, 8, ROWS), F32),
         pltpu.VMEM((2, BLOCKS, HALF, CC), BF16),
-        pltpu.VMEM((2, BLOCKS, 2, HALF, FF), BF16),
-        pltpu.VMEM((2, 2, 2, 2, QUARTER, FF), BF16),
-        pltpu.VMEM((2, 2, 2, 2, HALF, FF), BF16),
-        pltpu.VMEM((2, 2, HALF, FF), BF16),
+        pltpu.VMEM((2, BLOCKS, 2, HALF, WIDE), BF16),
+        pltpu.VMEM((2, 2, 2, 2, QUARTER, WIDE), BF16),
+        pltpu.VMEM((2, 2, 2, 2, HALF, WIDE), BF16),
+        pltpu.VMEM((2, 2, HALF, WIDE), BF16),
         pltpu.VMEM((2, BLOCKS, HALF, FF), BF16),
         *stages(),
+        pltpu.VMEM((FF, CC), BF16),
         pltpu.VMEM((2, HALF, CC), F32),
         pltpu.VMEM((CC, ROWS), BF16),
         pltpu.VMEM((COLS, ROWS), BF16),
@@ -838,7 +810,7 @@
             jax.ShapeDtypeStruct(queries.shape, BF16),
             jax.ShapeDtypeStruct(residual.shape[::-1], BF16),
         ),
-        in_specs=[vmem, hbm, hbm, vmem, vmem, vmem, vmem, smem, hbm, hbm, hbm, hbm, hbm, hbm],
+        in_specs=[vmem, hbm, hbm, vmem, vmem, vmem, vmem, smem, hbm, hbm, vmem, hbm, hbm, hbm],
         out_specs=(vmem, vmem),
         scratch_shapes=scratch,
         compiler_params=pltpu.CompilerParams(

time: 205 us -> 193 us (0.941)
  Pallas kernels: 198 us -> 184 us
    pallas_call x1, Pallas kernels: 198 us -> 184 us  [local(): pl.pallas_call(layer_kernel, out_shape=(jax.ShapeDtypeStruct(queries.shap...]
where the time goes in v3:
time: 193 us; the launch traced here: 189 us
  Pallas kernels  184 us (95%)
  local copies, waits for them, and re-layouts  4.38 us (2%)
    pallas_call x1, Pallas kernels, local(): pl.pallas_call(layer_kernel, out_shape=(jax.ShapeDtypeStruct(queries.shap...  184 us

profile of v3, /device:TPU:16, one launch (start us, length us, event | category | flops | bytes accessed | tf_op | source)
XLA Modules:
  0.0 189.3 jit_solution(4723789067623448329)
XLA Ops:
  0.6 1.3 broadcast_in_dim.2.gain_ref
  1.9 184.3 %layer.1 = (bf16[128,384]{1,0:T(8,128)(2,1)}, bf16[448,128]{1,0:T(8,128)(2,1)}) custom-call(bf16[128,384]{1,0:T(8,128)(2,1)} %q_ref.1, bf16[256,1024]{1,0:T(8,128)(2,1)} %key_ref.1, bf16[256,1024]{1,0:T(8,128)(2,1)} %value_ref.1, s32[16,128]{1,0:T(8,128)} %bitcast.14, s32[16,128]{1,0:T(8,128)} %bitcast.15, s32[32,128]{1,0:T(8,128)} %bitcast.12, ...), custom_call_target="tpu_custom_call" | custom-call | flops 8999999488 | bytes 8000000 | tf_op jit(solution)/shard_map/layer/pallas_call | solution.py:807
  186.3 1.5 copy.18
  187.8 1.6 copy.19

commit v4 on v3

--- a/solution.py
+++ b/solution.py
@@ -23,7 +23,7 @@
 COLS = 448
 CC = 2 * COLS
 FF = 1200
-WIDE = 1280
+WIDE = 2432
 BLOCKS = 8
 
 BLOCKED = -1e30
@@ -183,41 +183,6 @@
     send(own, own, down_y, ids[2])
     send(own, own, sibling, ids[3])
 
-    for one in loads[2:]:
-        one.wait()
-    gain = jnp.broadcast_to(gain_ref[0:1, :], (DH, COLS)).T[:, 0:1]
-    for weights in (wg2, wu2):
-        weights[my_rows] = (weights[my_rows].astype(F32) * gain).astype(BF16)
-
-    other = block_at(y, zo, k)
-    arrived(other, ids[0])
-    send(other, other, up_y, ids[4])
-    send(other, other, down_y, ids[5])
-    send(other, other, sibling, ids[6])
-    b = block_at(ym, z, k)
-    arrived(b, ids[1])
-    send(half_at(ym, z, k, 0), half_at(ym, z, k, 0), up_y, ids[7])
-    send(b, b, sibling, ids[9])
-    b = block_at(yp, z, k)
-    arrived(b, ids[2])
-    send(half_at(yp, z, k, 1), half_at(yp, z, k, 1), down_y, ids[8])
-    send(b, b, sibling, ids[10])
-    b = block_at(ym, zo, k)
-    arrived(b, ids[4])
-    send(half_at(ym, zo, k, 0), half_at(ym, zo, k, 0), up_y, ids[11])
-    send(b, b, sibling, ids[13])
-    b = block_at(yp, zo, k)
-    arrived(b, ids[5])
-    send(half_at(yp, zo, k, 1), half_at(yp, zo, k, 1), down_y, ids[12])
-    send(b, b, sibling, ids[14])
-
-    weight_id = numbers(5)
-    half_rows = pl.ds(pl.multiple_of(k * COLS, COLS), COLS)
-    other_rows = pl.ds(pl.multiple_of(ko * COLS, COLS), COLS)
-    joint = (wo2, res2, wg2, wu2, wd2)
-    for n, weights in enumerate(joint):
-        send(weights.at[half_rows], weights.at[half_rows], sibling, weight_id(n))
-
     for h in range(NH):
         q3[h] = q_ref[:, h * DH : (h + 1) * DH]
     m_s[...] = jnp.full(m_s.shape, BLOCKED, F32)
@@ -280,10 +245,47 @@
 
         lax.fori_loop(0, NH, one_head, 0)
 
+    for one in loads[2:]:
+        one.wait()
+    gain = jnp.broadcast_to(gain_ref[0:1, :], (DH, COLS)).T[:, 0:1]
+    for weights in (wg2, wu2):
+        weights[my_rows] = (weights[my_rows].astype(F32) * gain).astype(BF16)
+
+    other = block_at(y, zo, k)
+    arrived(other, ids[0])
+    send(other, other, up_y, ids[4])
+    send(other, other, down_y, ids[5])
+    send(other, other, sibling, ids[6])
+    b = block_at(ym, z, k)
+    arrived(b, ids[1])
+    send(half_at(ym, z, k, 0), half_at(ym, z, k, 0), up_y, ids[7])
+    send(b, b, sibling, ids[9])
+    b = block_at(yp, z, k)
+    arrived(b, ids[2])
+    send(half_at(yp, z, k, 1), half_at(yp, z, k, 1), down_y, ids[8])
+    send(b, b, sibling, ids[10])
     arrived(block_at(y, z, ko), ids[3])
     arrived(block_at(y, zo, ko), ids[6])
     attend(y)
 
+
+    b = block_at(ym, zo, k)
+    arrived(b, ids[4])
+    send(half_at(ym, zo, k, 0), half_at(ym, zo, k, 0), up_y, ids[11])
+    send(b, b, sibling, ids[13])
+    b = block_at(yp, zo, k)
+    arrived(b, ids[5])
+    send(half_at(yp, zo, k, 1), half_at(yp, zo, k, 1), down_y, ids[12])
+    send(b, b, sibling, ids[14])
+
+    weight_id = numbers(5)
+    half_rows = pl.ds(pl.multiple_of(k * COLS, COLS), COLS)
+    other_rows = pl.ds(pl.multiple_of(ko * COLS, COLS), COLS)
+    joint = (wo2, res2, wg2, wu2, wd2)
+
+    arrived(block_at(ym, z, ko), ids[9])
+    arrived(block_at(ym, zo, ko), ids[13])
+    attend(ym)
     arrived(half_at(yo, z, k, 0), ids[7])
     arrived(half_at(yo, z, k, 1), ids[8])
     b = block_at(yo, z, k)
@@ -292,10 +294,9 @@
     arrived(half_at(yo, zo, k, 1), ids[12])
     b = block_at(yo, zo, k)
     send(b, b, sibling, ids[16])
-
-    arrived(block_at(ym, z, ko), ids[9])
-    arrived(block_at(ym, zo, ko), ids[13])
-    attend(ym)
+    for n, weights in enumerate(joint):
+        send(weights.at[half_rows], weights.at[half_rows], sibling, weight_id(n))
+
     arrived(block_at(yp, z, ko), ids[10])
     arrived(block_at(yp, zo, ko), ids[14])
     attend(yp)
@@ -306,7 +307,9 @@
     mine = 2 * y + z
     for h in range(NH):
         total = jnp.sum(l_s[h], axis=1, keepdims=True)
-        att[mine, :, h * DH : (h + 1) * DH] = (acc_s[h] / total).astype(BF16)
+        rows = (acc_s[h] / total).astype(BF16)
+        for half in range(2):
+            att[half, mine, :, h * DH : (h + 1) * DH] = rows[half * HALF : (half + 1) * HALF]
 
     def gather_context(whole, piece, id_at, ready):
         own = whole(y, z)
@@ -443,33 +446,36 @@
 
     projected = Scatter(part, half_in, full_in, z_out, z_in, total_s)
     arrived(wo2.at[other_rows], weight_id(0))
-    seen = []
-    relay_a, flush_a = lagged(2, lambda to, j: projected.relay(0, to, j))
-
-    def project(to, j):
-        i = 2 * to + j
-        rows = lax.dot_general(
-            att[i], wo2[...], (((1,), (1,)), ((), ())), preferred_element_type=F32
-        ).astype(BF16)
-        part[0, i] = rows[:HALF]
-        part[1, i] = rows[HALF:]
-        projected.ready(0, to, j)
-        seen.append((to, j))
-        relay_a(to, j)
-
-    for _ in gather_context(
-        lambda y_, z_: att.at[2 * y_ + z_],
-        lambda y_, z_, h: att.at[2 * y_ + z_, h * HALF : (h + 1) * HALF],
-        numbers(9),
-        project,
-    ):
+    def spread_attention(h):
+        relay, flush = lagged(2, lambda to, j: projected.relay(h, to, j))
+
+        def project(to, j):
+            i = 2 * to + j
+            part[h, i] = lax.dot_general(
+                att[h, i], wo2[...], (((1,), (1,)), ((), ())), preferred_element_type=F32
+            ).astype(BF16)
+            projected.ready(h, to, j)
+            relay(to, j)
+
+        yield from gather_context(
+            lambda y_, z_: att.at[h, 2 * y_ + z_],
+            lambda y_, z_, q: att.at[h, 2 * y_ + z_, q * QUARTER : (q + 1) * QUARTER],
+            numbers(9),
+            project,
+        )
+        flush()
+
+    rows_a, rows_b = spread_attention(0), spread_attention(1)
+    next(rows_a)
+    next(rows_b)
+    for _ in rows_a:
         pass
-    for to, j in seen:
-        projected.ready(1, to, j)
-    flush_a()
-    for to, j in seen:
-        projected.relay(1, to, j)
-    att_out[...] = att[mine]
+    for _ in rows_b:
+        pass
+    arrived(wd2.at[other_rows], weight_id(4))
+    wd_t[...] = wd2[...].T
+    for h in range(2):
+        att_out[h * HALF : (h + 1) * HALF] = att[h, mine]
 
     gather_z_id = numbers(2, 3)
     gather_x_id = numbers(2, 4, 2)
@@ -516,7 +522,7 @@
     def y_half(h, zz, way):
         rows = slice(way * QUARTER, (way + 1) * QUARTER)
         return copy(
-            gu.at[h, 2 * yo + zz, :, rows],
+            gu.at[h, 2 * yo + zz, rows],
             gu_half.at[h, way, zz],
             (up_y, down_y)[way],
             half_id(h, zz, way),
@@ -537,10 +543,11 @@
         i = 2 * zq + j
         rows = normed[h, i]
         wide = rows.astype(F32)
-        squares = jnp.broadcast_to(jnp.sum(wide * wide, axis=1, keepdims=True), (HALF, WIDE - FF))
+        squares = jnp.sum(wide * wide, axis=1, keepdims=True)
+        squares = jnp.broadcast_to(squares, (HALF, WIDE - 2 * FF))
         gate = jnp.dot(rows, wg2[...], preferred_element_type=F32)
-        gu[h, i, 0] = jnp.concatenate([gate, squares], axis=1).astype(BF16)
-        gu[h, i, 1, :, :FF] = jnp.dot(rows, wu2[...], preferred_element_type=F32).astype(BF16)
+        up = jnp.dot(rows, wu2[...], preferred_element_type=F32)
+        gu[h, i] = jnp.concatenate([gate, up, squares], axis=1).astype(BF16)
 
         @pl.when(lax.rem(zq - y + 4, 4) == 2)
         def _():
@@ -590,33 +597,31 @@
                 for zz in (zo, z):
                     i = 2 * there + zz
                     arrived(gu_half.at[h, way, zz], half_id(h, zz, way))
-                    gu[h, i, :, rows] = (
-                        gu[h, i, :, rows].astype(F32) + gu_half[h, way, zz].astype(F32)
+                    gu[h, i, rows] = (
+                        gu[h, i, rows].astype(F32) + gu_half[h, way, zz].astype(F32)
                     ).astype(BF16)
                     y_full(h, zz, way).start()
 
-    def own_sum(h, zz, which):
+    def own_sum(h, zz):
         return (
-            gu[h, 2 * y + zz, which].astype(F32)
-            + gu_full[h, 0, zz, which].astype(F32)
-            + gu_full[h, 1, zz, which].astype(F32)
+            gu[h, 2 * y + zz].astype(F32)
+            + gu_full[h, 0, zz].astype(F32)
+            + gu_full[h, 1, zz].astype(F32)
         )
 
     def finish_y_across(h):
         arrived(gu_full.at[h, 0, zo], full_id(h, zo, 0))
         arrived(gu_full.at[h, 1, zo], full_id(h, zo, 1))
-        for which in range(2):
-            gu[h, 2 * y + zo, which] = own_sum(h, zo, which).astype(BF16)
+        gu[h, 2 * y + zo] = own_sum(h, zo).astype(BF16)
         y_cross(h).start()
 
     def finish_y(h):
         arrived(gu_full.at[h, 0, z], full_id(h, z, 0))
         arrived(gu_full.at[h, 1, z], full_id(h, z, 1))
         arrived(gu_z.at[h], cross_id(h))
-        gate = own_sum(h, z, 0) + gu_z[h, 0].astype(F32)
-        up = (own_sum(h, z, 1) + gu_z[h, 1].astype(F32))[:, :FF]
-        scale = lax.rsqrt(gate[:, FF : FF + 1] / D + 1e-05)
-        gate, up = gate[:, :FF] * scale, up * scale
+        total = own_sum(h, z) + gu_z[h].astype(F32)
+        scale = lax.rsqrt(total[:, 2 * FF : 2 * FF + 1] / D + 1e-05)
+        gate, up = total[:, :FF] * scale, total[:, FF : 2 * FF] * scale
         hid[h, mine] = (gate / (1.0 + jnp.exp(-gate)) * up).astype(BF16)
 
     def steps_a(n, carry):
@@ -624,7 +629,7 @@
         def _():
             take_first(0, n)
 
-        @pl.when(is_home & (n == 1))
+        @pl.when(is_home & (n == 3))
         def _():
             make_stream(1)
 
@@ -655,8 +660,6 @@
 
     lax.fori_loop(0, 5, steps_a, 0)
     lax.fori_loop(0, 5, steps_b, 0)
-    arrived(wd2.at[other_rows], weight_id(4))
-    wd_t[...] = wd2[...].T
     finish_y_across(0)
     for n in range(4):
         y_relay(1, n)
@@ -687,38 +690,12 @@
     for _ in spread_a:
         pass
     finish_y(1)
+    earlier = list(sent)
+    sent.clear()
     next(spread_b)
-
-    @pl.when(is_home)
-    def _():
-        summed.finish_x(0)
-
-    for _ in spread_b:
-        pass
-
-    mix_id = numbers(1)(0)
-    mix_mine = mix_t.at[other_rows]
-
-    @pl.when(is_home)
-    def _():
-        mixed_s[0] = normed[0, 2 * zl + home_j].astype(F32) + summed.finish_z(0)
-        summed.finish_x(1)
-        mixed_s[1] = normed[1, 2 * zl + home_j].astype(F32) + summed.finish_z(1)
-        mixed = jnp.concatenate([mixed_s[0], mixed_s[1]], axis=0)
-        mix_t[...] = mixed.T.astype(BF16)
-        copy(mix_mine, mix_recv, sibling, mix_id).start()
-        mix_out[...] = mix_t[half_rows]
-        copy(mix_mine, mix_recv, sibling, mix_id).wait_send()
-
-    @pl.when(is_relay)
-    def _():
-        arrived(mix_recv, mix_id)
-        mix_out[...] = mix_recv[...]
-
-    for one in sent:
+    for one in earlier:
         one.wait_send()
     projected.wait_sends()
-    summed.wait_sends()
     for h in range(2):
         for zz in range(2):
             for way in range(2):
@@ -742,6 +719,33 @@
                 for way in range(2):
                     gather_half(h, zq, way).wait_send()
 
+
+    for _ in spread_b:
+        pass
+
+    mix_id = numbers(1)(0)
+    mix_mine = mix_t.at[other_rows]
+
+    @pl.when(is_home)
+    def _():
+        summed.finish_x(0)
+        summed.finish_x(1)
+        mixed_s[0] = normed[0, 2 * zl + home_j].astype(F32) + summed.finish_z(0)
+        mixed_s[1] = normed[1, 2 * zl + home_j].astype(F32) + summed.finish_z(1)
+        mixed = jnp.concatenate([mixed_s[0], mixed_s[1]], axis=0)
+        mix_t[...] = mixed.T.astype(BF16)
+        copy(mix_mine, mix_recv, sibling, mix_id).start()
+        mix_out[...] = mix_t[half_rows]
+        copy(mix_mine, mix_recv, sibling, mix_id).wait_send()
+
+    @pl.when(is_relay)
+    def _():
+        arrived(mix_recv, mix_id)
+        mix_out[...] = mix_recv[...]
+
+    for one in sent:
+        one.wait_send()
+    summed.wait_sends()
     assert count[0] <= N_COPIES
 
 
@@ -781,7 +785,7 @@
         pltpu.VMEM((NH, ROWS, DH), F32),
         pltpu.VMEM((NH, ROWS, DH), F32),
         pltpu.VMEM((NH, ROWS, DH), F32),
-        pltpu.VMEM((BLOCKS, ROWS, NH * DH), BF16),
+        pltpu.VMEM((2, BLOCKS, HALF, NH * DH), BF16),
         pltpu.VMEM((CC, NH * DH), BF16),
         pltpu.VMEM((CC, FF), BF16),
         pltpu.VMEM((CC, FF), BF16),
@@ -790,10 +794,10 @@
         pltpu.VMEM((2, HALF, CC), F32),
         *stages(),
         pltpu.VMEM((2, BLOCKS, HALF, CC), BF16),
-        pltpu.VMEM((2, BLOCKS, 2, HALF, WIDE), BF16),
-        pltpu.VMEM((2, 2, 2, 2, QUARTER, WIDE), BF16),
-        pltpu.VMEM((2, 2, 2, 2, HALF, WIDE), BF16),
-        pltpu.VMEM((2, 2, HALF, WIDE), BF16),
+        pltpu.VMEM((2, BLOCKS, HALF, WIDE), BF16),
+        pltpu.VMEM((2, 2, 2, QUARTER, WIDE), BF16),
+        pltpu.VMEM((2, 2, 2, HALF, WIDE), BF16),
+        pltpu.VMEM((2, HALF, WIDE), BF16),
         pltpu.VMEM((2, BLOCKS, HALF, FF), BF16),
         *stages(),
         pltpu.VMEM((FF, CC), BF16),

time: 193 us -> 186 us (0.964); the launches traced: 189 us -> 186 us
  Pallas kernels: 184 us -> 181 us
    pallas_call x1, Pallas kernels: 184 us -> 181 us  [local(): pl.pallas_call(layer_kernel, out_shape=(jax.ShapeDtypeStruct(queries.shap...]
where the time goes in v4:
time: 186 us
  Pallas kernels  181 us (97%)
  local copies, waits for them, and re-layouts  4.38 us (2%)
    pallas_call x1, Pallas kernels, local(): pl.pallas_call(layer_kernel, out_shape=(jax.ShapeDtypeStruct(queries.shap...  181 us

profile of v4, /device:TPU:16, one launch (start us, length us, event | category | flops | bytes accessed | tf_op | source)
XLA Modules:
  0.0 185.6 jit_solution(15149090111764982101)
XLA Ops:
  0.6 1.3 broadcast_in_dim.2.gain_ref
  1.9 180.6 %layer.1 = (bf16[128,384]{1,0:T(8,128)(2,1)}, bf16[448,128]{1,0:T(8,128)(2,1)}) custom-call(bf16[128,384]{1,0:T(8,128)(2,1)} %q_ref.1, bf16[256,1024]{1,0:T(8,128)(2,1)} %key_ref.1, bf16[256,1024]{1,0:T(8,128)(2,1)} %value_ref.1, s32[16,128]{1,0:T(8,128)} %bitcast.14, s32[16,128]{1,0:T(8,128)} %bitcast.15, s32[32,128]{1,0:T(8,128)} %bitcast.12, ...), custom_call_target="tpu_custom_call" | custom-call | flops 8999999488 | bytes 8000000 | tf_op jit(solution)/shard_map/layer/pallas_call | solution.py:811
  182.5 1.5 copy.18
  184.0 1.6 copy.19

commit v5 on v4

--- a/solution.py
+++ b/solution.py
@@ -652,6 +652,10 @@
         def _():
             y_relay(0, n + 2)
 
+        @pl.when(n == 4)
+        def _():
+            finish_y_across(0)
+
         @pl.when(n >= 1)
         def _():
             take_second(1, n - 1)
@@ -660,7 +664,6 @@
 
     lax.fori_loop(0, 5, steps_a, 0)
     lax.fori_loop(0, 5, steps_b, 0)
-    finish_y_across(0)
     for n in range(4):
         y_relay(1, n)
 

time: 186 us -> 184 us (0.989)
  Pallas kernels: 181 us -> 178 us
    pallas_call x1, Pallas kernels: 181 us -> 178 us  [local(): pl.pallas_call(layer_kernel, out_shape=(jax.ShapeDtypeStruct(queries.shap...]
where the time goes in v5:
time: 184 us; the launch traced here: 183 us
  Pallas kernels  178 us (97%)
  local copies, waits for them, and re-layouts  4.38 us (2%)
    pallas_call x1, Pallas kernels, local(): pl.pallas_call(layer_kernel, out_shape=(jax.ShapeDtypeStruct(queries.shap...  178 us

profile of v5, /device:TPU:16, one launch (start us, length us, event | category | flops | bytes accessed | tf_op | source)
XLA Modules:
  0.0 182.8 jit_solution(7808197848823775477)
XLA Ops:
  0.6 1.3 broadcast_in_dim.2.gain_ref
  1.9 177.8 %layer.1 = (bf16[128,384]{1,0:T(8,128)(2,1)}, bf16[448,128]{1,0:T(8,128)(2,1)}) custom-call(bf16[128,384]{1,0:T(8,128)(2,1)} %q_ref.1, bf16[256,1024]{1,0:T(8,128)(2,1)} %key_ref.1, bf16[256,1024]{1,0:T(8,128)(2,1)} %value_ref.1, s32[16,128]{1,0:T(8,128)} %bitcast.14, s32[16,128]{1,0:T(8,128)} %bitcast.15, s32[32,128]{1,0:T(8,128)} %bitcast.12, ...), custom_call_target="tpu_custom_call" | custom-call | flops 8999999488 | bytes 8000000 | tf_op jit(solution)/shard_map/layer/pallas_call | solution.py:814
  179.7 1.5 copy.18
  181.2 1.6 copy.19
